TPU v7x, 512 devices: a whole 4x4x16 slice. The times are simulated.
512 devices in a mesh: dp: 8 (over z_lo), tm: 8 (over x, core), space: 8 (over y, z_hi).
Axes of the slice: x: 4, y: 4, z: 16 (z_hi: 2, z_lo: 8; z = z_hi * 8 + z_lo), core: 2. Of those that a mesh axis runs over, the one named last changes fastest.
Arguments:
- queries: bfloat16 [64, 1536, 3072], P(('dp', 'tm'), 'space'), parts along dimension 0, may hold values from -70 to 70
- keys: bfloat16 [64, 1536, 3072], P(('dp', 'tm'), 'space'), parts along dimension 0, may hold values from -5 to 5
- values: bfloat16 [64, 1536, 3072], P(('dp', 'tm'), 'space'), parts along dimension 0, may hold values from -6 to 6
Outputs:
- attended: bfloat16 [64, 1536, 3072], P(('dp', 'tm'), 'space'), parts along dimension 0
There are 8 independent parts, one for each index of `dp`. A program takes and returns all parts, laid end to end along the dimension named above; each array names one. Nothing has to cross between parts.
All inputs are finite; a program needn't handle non-finite values.
Results may differ from a plain program's by a relative error of at most 0.0049.
Values may be sent and summed in bfloat16 or wider, within the bound.
No kernel may reach another device: no remote copies, remote signals or barrier semaphores. Data moves between devices by JAX's collectives and lax.ppermute only.
A program may use at most 64 MiB of HBM per device.

v0:
```python
import math

import jax
import jax.numpy as jnp
from jax import lax
from jax.sharding import PartitionSpec as P

HS = 16
HT = 8
DH = 128


def block_attention(query_block, key_head, value_head):
    scores = jnp.einsum(
        "rqd,rkd->rqk", query_block, key_head, preferred_element_type=jnp.float32
    ) * (1.0 / math.sqrt(DH))
    weights = jax.nn.softmax(scores, axis=-1).astype(jnp.bfloat16)
    output = jnp.einsum("rqk,rkd->rqd", weights, value_head, preferred_element_type=jnp.float32)
    return output.astype(jnp.bfloat16)


def frame_attention(query_all, key_all, value_all):
    frames_here, rows, heads_here, depth = query_all.shape
    block = 512

    def per_head(trio):
        query_head, key_head, value_head = trio
        blocks = jnp.moveaxis(query_head.reshape(frames_here, rows // block, block, depth), 1, 0)
        outputs = lax.map(
            lambda query_block: block_attention(query_block, key_head, value_head), blocks
        )
        return jnp.moveaxis(outputs, 0, 1).reshape(frames_here, rows, depth)

    heads_first = lax.map(
        per_head,
        (jnp.moveaxis(query_all, 2, 0), jnp.moveaxis(key_all, 2, 0), jnp.moveaxis(value_all, 2, 0)),
    )
    return jnp.moveaxis(heads_first, 0, 2)


def time_attention(trio):
    query_part, key_part, value_part = trio
    frames_all, unit_dim, tokens_here, width_time = query_part.shape
    shape = (frames_all, tokens_here, HT, DH)
    scores = jnp.einsum(
        "fmhd,gmhd->mhfg",
        query_part.reshape(shape),
        key_part.reshape(shape),
        preferred_element_type=jnp.float32,
    ) * (1.0 / math.sqrt(DH))
    weights = jax.nn.softmax(scores, axis=-1).astype(jnp.bfloat16)
    output = jnp.einsum(
        "mhfg,gmhd->fmhd", weights, value_part.reshape(shape), preferred_element_type=jnp.float32
    )
    return output.astype(jnp.bfloat16).reshape(frames_all, unit_dim, tokens_here, width_time)


def on_device(queries, keys, values):
    frames_loc, tok_loc, width = queries.shape
    space_count = lax.axis_size("space")
    time_count = lax.axis_size("tm")
    split = HS * DH
    per_device = HS // space_count

    def heads_view(array):
        return array[..., :split].reshape(frames_loc, tok_loc, space_count, per_device, DH)

    query_ex = lax.all_to_all(heads_view(queries), "space", split_axis=2, concat_axis=1, tiled=True)
    key_ex = lax.all_to_all(heads_view(keys), "space", split_axis=2, concat_axis=1, tiled=True)
    value_ex = lax.all_to_all(heads_view(values), "space", split_axis=2, concat_axis=1, tiled=True)
    rows = query_ex.shape[1]
    count_heads = query_ex.shape[3]
    shape = (frames_loc, rows, count_heads, DH)
    output = frame_attention(
        query_ex.reshape(shape), key_ex.reshape(shape), value_ex.reshape(shape)
    )
    regrouped = output.reshape(frames_loc, rows, 1, count_heads, DH)
    returned = lax.all_to_all(regrouped, "space", split_axis=1, concat_axis=2, tiled=True)
    spatial_block = returned.reshape(frames_loc, tok_loc, split)

    def time_view(array):
        return array[..., split:].reshape(
            frames_loc, time_count, tok_loc // time_count, width - split
        )

    regrouped = time_attention(
        (
            lax.all_to_all(time_view(queries), "tm", split_axis=1, concat_axis=0, tiled=True),
            lax.all_to_all(time_view(keys), "tm", split_axis=1, concat_axis=0, tiled=True),
            lax.all_to_all(time_view(values), "tm", split_axis=1, concat_axis=0, tiled=True),
        )
    )
    returned = lax.all_to_all(regrouped, "tm", split_axis=0, concat_axis=1, tiled=True)
    temporal_block = returned.reshape(frames_loc, tok_loc, width - split)
    return jnp.concatenate([spatial_block, temporal_block], axis=-1)


def solution(mesh):
    in_specs = (
        P(("dp", "tm"), "space", None),
        P(("dp", "tm"), "space", None),
        P(("dp", "tm"), "space", None),
    )
    out_specs = P(("dp", "tm"), "space", None)
    return jax.shard_map(
        on_device, mesh=mesh, in_specs=in_specs, out_specs=out_specs, check_vma=False
    )
```

profile of v0, /device:TPU:32, one launch (start us, length us, event | category | flops | bytes accessed | tf_op | source)
XLA Modules:
  0.0 241.3 jit_solution(7752492063296711163)
XLA Ops:
  0.0 1.8 slice.21
  1.8 4.3 %all-to-all-start.4 = ((bf16[1,8,24,1024]{3,2,0,1:T(8,128)(2,1)}), bf16[1,8,24,1024]{3,2,0,1:T(8,128)(2,1)S(1)}, u32[]{:S(2)}, u32[]{:S(2)}) async-start(bf16[1,8,24,1024]{3,2,0,1:T(8,128)(2,1)} %bitcast.27), calls=%async_computation.4 | async-start | bytes 786432 | tf_op jit(solution)/shard_map/all_to_all | solution.py:88
  6.7 1.1 copy.26
  7.8 7.3 %all-to-all-done.4 = bf16[1,8,24,1024]{3,2,0,1:T(8,128)(2,1)S(1)} async-done(((bf16[1,8,24,1024]{3,2,0,1:T(8,128)(2,1)}), bf16[1,8,24,1024]{3,2,0,1:T(8,128)(2,1)S(1)}, u32[]{:S(2)}, u32[]{:S(2)}) %all-to-all-start.4) | async-done | bytes 393248 | tf_op jit(solution)/shard_map/all_to_all | solution.py:88
  15.9 16.8 %all-to-all-start = ((bf16[1,192,8,2,128]{4,1,3,0,2:T(8,128)(2,1)}), bf16[1,192,8,2,128]{4,1,3,0,2:T(8,128)(2,1)S(1)}, u32[]{:S(2)}, u32[]{:S(2)}) async-start(bf16[1,192,8,2,128]{4,1,3,0,2:T(8,128)(2,1)} %copy.26), calls=%async_computation | async-start | bytes 1572864 | tf_op jit(solution)/shard_map/all_to_all | solution.py:68
  33.3 1.1 copy.28
  34.4 45.2 %all-to-all-done = bf16[1,192,8,2,128]{4,1,3,0,2:T(8,128)(2,1)S(1)} async-done(((bf16[1,192,8,2,128]{4,1,3,0,2:T(8,128)(2,1)}), bf16[1,192,8,2,128]{4,1,3,0,2:T(8,128)(2,1)S(1)}, u32[]{:S(2)}, u32[]{:S(2)}) %all-to-all-start) | async-done | bytes 786464 | tf_op jit(solution)/shard_map/all_to_all | solution.py:68
  79.6 3.5 %all-to-all-start.1 = ((bf16[1,192,8,2,128]{4,1,3,0,2:T(8,128)(2,1)}), bf16[1,192,8,2,128]{4,1,3,0,2:T(8,128)(2,1)S(1)}, u32[]{:S(2)}, u32[]{:S(2)}) async-start(bf16[1,192,8,2,128]{4,1,3,0,2:T(8,128)(2,1)} %copy.28), calls=%async_computation.1 | async-start | bytes 1572864 | tf_op jit(solution)/shard_map/all_to_all | solution.py:69
  83.2 1.2 slice.20
  85.0 1.1 copy.30
  86.0 27.3 %all-to-all-done.1 = bf16[1,192,8,2,128]{4,1,3,0,2:T(8,128)(2,1)S(1)} async-done(((bf16[1,192,8,2,128]{4,1,3,0,2:T(8,128)(2,1)}), bf16[1,192,8,2,128]{4,1,3,0,2:T(8,128)(2,1)S(1)}, u32[]{:S(2)}, u32[]{:S(2)}) %all-to-all-start.1) | async-done | bytes 786464 | tf_op jit(solution)/shard_map/all_to_all | solution.py:69
  113.4 11.6 %all-to-all-start.2 = ((bf16[1,192,8,2,128]{4,1,3,0,2:T(8,128)(2,1)}), bf16[1,192,8,2,128]{4,1,3,0,2:T(8,128)(2,1)S(1)}, u32[]{:S(2)}, u32[]{:S(2)}) async-start(bf16[1,192,8,2,128]{4,1,3,0,2:T(8,128)(2,1)} %copy.30), calls=%async_computation.2 | async-start | bytes 1572864 | tf_op jit(solution)/shard_map/all_to_all | solution.py:70
  125.0 1.8 slice.22
  126.8 29.7 %all-to-all-done.2 = bf16[1,192,8,2,128]{4,1,3,0,2:T(8,128)(2,1)S(1)} async-done(((bf16[1,192,8,2,128]{4,1,3,0,2:T(8,128)(2,1)}), bf16[1,192,8,2,128]{4,1,3,0,2:T(8,128)(2,1)S(1)}, u32[]{:S(2)}, u32[]{:S(2)}) %all-to-all-start.2) | async-done | bytes 786464 | tf_op jit(solution)/shard_map/all_to_all | solution.py:70
  156.4 3.5 %all-to-all-start.5 = ((bf16[1,8,24,1024]{3,2,0,1:T(8,128)(2,1)}), bf16[1,8,24,1024]{3,2,0,1:T(8,128)(2,1)S(1)}, u32[]{:S(2)}, u32[]{:S(2)}) async-start(bf16[1,8,24,1024]{3,2,0,1:T(8,128)(2,1)} %bitcast.28), calls=%async_computation.5 | async-start | bytes 786432 | tf_op jit(solution)/shard_map/all_to_all | solution.py:89
  159.9 1.8 slice.23
  161.8 0.9 copy.31
  162.7 6.0 %all-to-all-done.5 = bf16[1,8,24,1024]{3,2,0,1:T(8,128)(2,1)S(1)} async-done(((bf16[1,8,24,1024]{3,2,0,1:T(8,128)(2,1)}), bf16[1,8,24,1024]{3,2,0,1:T(8,128)(2,1)S(1)}, u32[]{:S(2)}, u32[]{:S(2)}) %all-to-all-start.5) | async-done | bytes 393248 | tf_op jit(solution)/shard_map/all_to_all | solution.py:89
  168.8 4.1 %all-to-all-start.6 = ((bf16[1,8,24,1024]{3,2,0,1:T(8,128)(2,1)}), bf16[1,8,24,1024]{3,2,0,1:T(8,128)(2,1)}, u32[]{:S(2)}, u32[]{:S(2)}) async-start(bf16[1,8,24,1024]{3,2,0,1:T(8,128)(2,1)} %bitcast.109), calls=%async_computation.6 | async-start | bytes 786432 | tf_op jit(solution)/shard_map/all_to_all | solution.py:90
  172.9 15.9 %while.21 = (s32[]{:T(128)}, bf16[2,1,1536,128]{3,2,1,0:T(8,128)(2,1)}, bf16[2,1,1536,128]{3,2,1,0:T(8,128)(2,1)S(1)}, bf16[2,1,1536,128]{3,2,1,0:T(8,128)(2,1)S...) while((s32[]{:T(128)}, bf16[2,1,1536,128]{3,2,1,0:T(8,128)(2,1)}, ...), condition=%wide.region_5.6_spmd, body=%wide.region_0.5_spmd.sunk | while | flops 408222720 | bytes 13642466 | solution.py:34
  172.9 1.1 dynamic-slice_bitcast_fusion.3
  174.0 6.1 %while.22 = (s32[]{:T(128)}, bf16[3,1,512,128]{3,2,1,0:T(8,128)(2,1)S(1)}, bf16[3,1,512,128]{3,2,1,0:T(8,128)(2,1)S(1)}, bf16[1,1536,128]{2,1,0:T(8,128)(2,1)S(1)}, bf16[1,1536,128]{2,1,0:T(8,128)(2,1)S(1)}, /*index=5*/s32[]{:T(128)}) while((s32[]{:T(128)}, bf16[3,1,512,128]{3,2,1,0:T(8,128)(2,1)S(1)}, bf16[3,1,512,128]{3,2,1,0:T(8,128)(2,1)S(1)}, ...), condition=%wide.region_4.4_spmd, body=%wide.region_1.3_spmd.sunk | while | flops 408222720 | bytes 10496077 | solution.py:29
  180.8 1.0 dynamic-slice_bitcast_fusion.3
  181.9 6.1 %while.22 = (s32[]{:T(128)}, bf16[3,1,512,128]{3,2,1,0:T(8,128)(2,1)S(1)}, bf16[3,1,512,128]{3,2,1,0:T(8,128)(2,1)S(1)}, bf16[1,1536,128]{2,1,0:T(8,128)(2,1)S(1)}, bf16[1,1536,128]{2,1,0:T(8,128)(2,1)S(1)}, /*index=5*/s32[]{:T(128)}) while((s32[]{:T(128)}, bf16[3,1,512,128]{3,2,1,0:T(8,128)(2,1)S(1)}, bf16[3,1,512,128]{3,2,1,0:T(8,128)(2,1)S(1)}, ...), condition=%wide.region_4.4_spmd, body=%wide.region_1.3_spmd.sunk | while | flops 408222720 | bytes 10496077 | solution.py:29
  188.8 7.5 %copy.62 = bf16[2,1,1536,128]{3,0,2,1:T(2,128)(2,1)} copy(bf16[2,1,1536,128]{3,2,1,0:T(8,128)(2,1)} %get-tuple-element.59) | data formatting | bytes 1572864 | tf_op jit(solution)/shard_map/while | solution.py:34
  196.3 3.5 %all-to-all-start.3 = ((bf16[1,1536,1,2,128]{4,3,2,0,1:T(2,128)(2,1)}), bf16[1,1536,1,2,128]{4,3,2,0,1:T(2,128)(2,1)S(1)}, u32[]{:S(2)}, u32[]{:S(2)}) async-start(bf16[1,1536,1,2,128]{4,3,2,0,1:T(2,128)(2,1)} %bitcast.87), calls=%async_computation.3 | async-start | bytes 1572864 | tf_op jit(solution)/shard_map/all_to_all | solution.py:78
  200.0 1.1 copy.46
  203.1 0.9 reshape.120
  204.1 22.8 %all-to-all-done.3 = bf16[1,1536,1,2,128]{4,3,2,0,1:T(2,128)(2,1)S(1)} async-done(((bf16[1,1536,1,2,128]{4,3,2,0,1:T(2,128)(2,1)}), bf16[1,1536,1,2,128]{4,3,2,0,1:T(2,128)(2,1)S(1)}, u32[]{:S(2)}, u32[]{:S(2)}) %all-to-all-start.3) | async-done | bytes 786464 | tf_op jit(solution)/shard_map/all_to_all | solution.py:78
  226.8 4.5 %all-to-all-start.7 = ((bf16[8,1,24,1024]{3,2,1,0:T(8,128)(2,1)}), bf16[8,1,24,1024]{3,2,1,0:T(8,128)(2,1)S(1)}, u32[]{:S(2)}, u32[]{:S(2)}) async-start(bf16[8,1,24,1024]{3,2,1,0:T(8,128)(2,1)} %bitcast.31), calls=%async_computation.7 | async-start | bytes 786432 | tf_op jit(solution)/shard_map/all_to_all | solution.py:93
  232.4 7.8 %all-to-all-done.7 = bf16[8,1,24,1024]{3,2,1,0:T(8,128)(2,1)S(1)} async-done(((bf16[8,1,24,1024]{3,2,1,0:T(8,128)(2,1)}), bf16[8,1,24,1024]{3,2,1,0:T(8,128)(2,1)S(1)}, u32[]{:S(2)}, u32[]{:S(2)}) %all-to-all-start.7) | async-done | bytes 393248 | tf_op jit(solution)/shard_map/all_to_all | solution.py:93
  240.2 1.1 pad_maximum_fusion
  (48 shorter events, 19.6 us)
Async XLA Ops:
  0.0 6.2 %slice-start = ((bf16[1,192,3072]{2,1,0:T(8,128)(2,1)}), bf16[1,192,2048]{2,1,0:T(8,128)(2,1)S(1)}, s32[]{:S(2)}) async-start(bf16[1,192,3072]{2,1,0:T(8,128)(2,1)} %param.7), calls=%async_computation.8 | async-start | bytes 1572864 | tf_op jit(solution)/shard_map/slice | solution.py:66
  1.8 13.2 %all-to-all-start.4 = ((bf16[1,8,24,1024]{3,2,0,1:T(8,128)(2,1)}), bf16[1,8,24,1024]{3,2,0,1:T(8,128)(2,1)S(1)}, u32[]{:S(2)}, u32[]{:S(2)}) async-start(bf16[1,8,24,1024]{3,2,0,1:T(8,128)(2,1)} %bitcast.27), calls=%async_computation.4 | async-start | bytes 786432 | tf_op jit(solution)/shard_map/all_to_all | solution.py:88
  6.1 26.5 %copy-start.2 = (bf16[1,192,3072]{2,1,0:T(8,128)(2,1)S(1)}, bf16[1,192,3072]{2,1,0:T(8,128)(2,1)}, u32[]{:S(2)}) copy-start(bf16[1,192,3072]{2,1,0:T(8,128)(2,1)} %param.8) | copy-start | bytes 3538948
  15.1 0.8 copy-start
  15.9 63.8 %all-to-all-start = ((bf16[1,192,8,2,128]{4,1,3,0,2:T(8,128)(2,1)}), bf16[1,192,8,2,128]{4,1,3,0,2:T(8,128)(2,1)S(1)}, u32[]{:S(2)}, u32[]{:S(2)}) async-start(bf16[1,192,8,2,128]{4,1,3,0,2:T(8,128)(2,1)} %copy.26), calls=%async_computation | async-start | bytes 1572864 | tf_op jit(solution)/shard_map/all_to_all | solution.py:68
  79.6 33.7 %all-to-all-start.1 = ((bf16[1,192,8,2,128]{4,1,3,0,2:T(8,128)(2,1)}), bf16[1,192,8,2,128]{4,1,3,0,2:T(8,128)(2,1)S(1)}, u32[]{:S(2)}, u32[]{:S(2)}) async-start(bf16[1,192,8,2,128]{4,1,3,0,2:T(8,128)(2,1)} %copy.28), calls=%async_computation.1 | async-start | bytes 1572864 | tf_op jit(solution)/shard_map/all_to_all | solution.py:69
  113.4 43.0 %all-to-all-start.2 = ((bf16[1,192,8,2,128]{4,1,3,0,2:T(8,128)(2,1)}), bf16[1,192,8,2,128]{4,1,3,0,2:T(8,128)(2,1)S(1)}, u32[]{:S(2)}, u32[]{:S(2)}) async-start(bf16[1,192,8,2,128]{4,1,3,0,2:T(8,128)(2,1)} %copy.30), calls=%async_computation.2 | async-start | bytes 1572864 | tf_op jit(solution)/shard_map/all_to_all | solution.py:70
  156.4 12.3 %all-to-all-start.5 = ((bf16[1,8,24,1024]{3,2,0,1:T(8,128)(2,1)}), bf16[1,8,24,1024]{3,2,0,1:T(8,128)(2,1)S(1)}, u32[]{:S(2)}, u32[]{:S(2)}) async-start(bf16[1,8,24,1024]{3,2,0,1:T(8,128)(2,1)} %bitcast.28), calls=%async_computation.5 | async-start | bytes 786432 | tf_op jit(solution)/shard_map/all_to_all | solution.py:89
  168.8 27.5 %all-to-all-start.6 = ((bf16[1,8,24,1024]{3,2,0,1:T(8,128)(2,1)}), bf16[1,8,24,1024]{3,2,0,1:T(8,128)(2,1)}, u32[]{:S(2)}, u32[]{:S(2)}) async-start(bf16[1,8,24,1024]{3,2,0,1:T(8,128)(2,1)} %bitcast.109), calls=%async_computation.6 | async-start | bytes 786432 | tf_op jit(solution)/shard_map/all_to_all | solution.py:90
  188.8 11.0 %copy-start.1 = (bf16[1,8,24,1024]{3,2,0,1:T(8,128)(2,1)S(1)}, bf16[1,8,24,1024]{3,2,0,1:T(8,128)(2,1)}, u32[]{:S(2)}) copy-start(bf16[1,8,24,1024]{3,2,0,1:T(8,128)(2,1)} %copy-done) | copy-start | bytes 1179652
  196.3 30.6 %all-to-all-start.3 = ((bf16[1,1536,1,2,128]{4,3,2,0,1:T(2,128)(2,1)}), bf16[1,1536,1,2,128]{4,3,2,0,1:T(2,128)(2,1)S(1)}, u32[]{:S(2)}, u32[]{:S(2)}) async-start(bf16[1,1536,1,2,128]{4,3,2,0,1:T(2,128)(2,1)} %bitcast.87), calls=%async_computation.3 | async-start | bytes 1572864 | tf_op jit(solution)/shard_map/all_to_all | solution.py:78
  226.8 13.4 %all-to-all-start.7 = ((bf16[8,1,24,1024]{3,2,1,0:T(8,128)(2,1)}), bf16[8,1,24,1024]{3,2,1,0:T(8,128)(2,1)S(1)}, u32[]{:S(2)}, u32[]{:S(2)}) async-start(bf16[8,1,24,1024]{3,2,1,0:T(8,128)(2,1)} %bitcast.31), calls=%async_computation.7 | async-start | bytes 786432 | tf_op jit(solution)/shard_map/all_to_all | solution.py:93
where the time goes:
time: 242 us; the launch traced here: 241 us
  waiting for transfers between devices  146 us (60%)
  starting transfers between devices  51.8 us (21%)
  local copies, waits for them, and re-layouts  27.9 us (12%)
  matrix products  10.6 us (4%)
  other arithmetic  4.55 us (2%)
    all_to_all x1, waiting for transfers between devices, on_device(): lax.all_to_all(heads_view(queries), 'space', split_axis=2, concat_axis=1,...  45.2 us
    all_to_all x1, waiting for transfers between devices, on_device(): lax.all_to_all(heads_view(values), 'space', split_axis=2, concat_axis=1,...  29.7 us
    all_to_all x1, waiting for transfers between devices, on_device(): lax.all_to_all(heads_view(keys), 'space', split_axis=2, concat_axis=1, ti...  27.3 us
    all_to_all x1, waiting for transfers between devices, on_device(): lax.all_to_all(regrouped, 'space', split_axis=1, concat_axis=2, tiled=True)  22.8 us
    all_to_all x1, starting transfers between devices, on_device(): lax.all_to_all(heads_view(queries), 'space', split_axis=2, concat_axis=1,...  16.8 us
    all_to_all x1, starting transfers between devices, on_device(): lax.all_to_all(heads_view(values), 'space', split_axis=2, concat_axis=1,...  11.6 us
    all_to_all x1, waiting for transfers between devices, on_device(): lax.all_to_all(regrouped, 'tm', split_axis=0, concat_axis=1, tiled=True)  7.8 us
    while x1, local copies, waits for them, and re-layouts, frame_attention(): lax.map(per_head, (jnp.moveaxis(query_all, 2, 0), jnp.moveaxis(key_all, 2...  7.47 us
  transfers between devices with their start and end apart: 8, of which 7 were waited for; matrix products, arithmetic and copies ran while one was open for 16% of the time, Pallas kernels for 0%

commit v1 on v0

v1 whole, which is shorter than its diff:
```python
import math

import jax
import jax.numpy as jnp
from jax import lax
from jax.experimental import pallas as pl
from jax.experimental.pallas import tpu as pltpu
from jax.sharding import Mesh, PartitionSpec as P

HS = 16
HT = 8
DH = 128
Y = 4
CH = HS // Y
SCALE = 1.0 / math.sqrt(DH)
SCALE2 = SCALE * math.log2(math.e)
ANY = pl.BlockSpec(memory_space=pl.ANY)
VMEM_LIMIT = 60 * 1024 * 1024
COST = pl.CostEstimate(flops=0, bytes_accessed=0, transcendentals=0)


def params(limit=VMEM_LIMIT):
    return pltpu.CompilerParams(vmem_limit_bytes=limit)


def whole(shape):
    return pl.BlockSpec(shape, lambda i: (0,) * len(shape))


def pack(sources, out_shapes, plan, after=()):
    rows, count, skip = sources[0][0].shape[1], len(sources), len(after)

    def body(*refs):
        for source, y, o, index in plan:
            refs[count + skip + o][index] = refs[source][0, :, pl.ds(y * DH, DH)]

    return pl.pallas_call(
        body,
        grid=(1,),
        out_shape=[jax.ShapeDtypeStruct(s, jnp.bfloat16) for s in out_shapes],
        in_specs=[
            pl.BlockSpec((1, rows, Y * DH), lambda i, g=group: (0, 0, g)) for _, group in sources
        ]
        + [ANY] * skip,
        out_specs=[whole(s) for s in out_shapes],
        compiler_params=params(),
        cost_estimate=COST,
    )(*[array for array, _ in sources], *after)


def unpack(pieces, plan, rows, width, base=None):
    count = len(pieces)
    extra = 0 if base is None else 1
    groups = [group for group, _ in plan]

    def column(i):
        place = jnp.int32(groups[0])
        for n, group in enumerate(groups):
            place = jnp.where(i == n, group, place)
        return place

    def body(*refs):
        out = refs[count + extra]
        for n, (_, heads) in enumerate(plan):

            @pl.when(pl.program_id(0) == n)
            def _write(heads=heads):
                for y, (p, index) in enumerate(heads):
                    out[0, :, pl.ds(y * DH, DH)] = refs[p][index]

    return pl.pallas_call(
        body,
        grid=(len(plan),),
        out_shape=jax.ShapeDtypeStruct((1, rows, width), jnp.bfloat16),
        in_specs=[whole(p.shape) for p in pieces] + [ANY] * extra,
        out_specs=pl.BlockSpec((1, rows, Y * DH), lambda i: (0, 0, column(i))),
        input_output_aliases={} if base is None else {count: 0},
        compiler_params=params(),
        cost_estimate=COST,
    )(*pieces, *([] if base is None else [base]))


def scores_of(q, k):
    return lax.dot_general(q, k, (((1,), (1,)), ((), ())), preferred_element_type=jnp.float32)


def attend_body(q_ref, kl_ref, vl_ref, kr_ref, vr_ref, *rest):
    o_ref = rest[-1]
    rows = q_ref.shape[2]

    def flat(ref):
        return ref[...].reshape(Y * rows, DH)

    q = q_ref[0, 0]
    sl = scores_of(q, flat(kl_ref))
    sr = scores_of(q, flat(kr_ref))
    top = jnp.maximum(sl.max(axis=-1, keepdims=True), sr.max(axis=-1, keepdims=True))
    wl = jnp.exp2((sl - top) * SCALE2)
    wr = jnp.exp2((sr - top) * SCALE2)
    total = wl.sum(axis=-1, keepdims=True) + wr.sum(axis=-1, keepdims=True)
    out = jnp.dot(wl.astype(jnp.bfloat16), flat(vl_ref), preferred_element_type=jnp.float32)
    out += jnp.dot(wr.astype(jnp.bfloat16), flat(vr_ref), preferred_element_type=jnp.float32)
    o_ref[0, 0] = (out / total).astype(jnp.bfloat16)


def attend(query, near, far, slots, slot, base=None, after=()):
    rows = query[0].shape[2]

    def part(source, more):
        return pl.BlockSpec((Y, 1, rows, DH), lambda i: (0, source[1] + more, 0, 0))

    extra = [] if base is None else [base]
    return pl.pallas_call(
        attend_body,
        grid=(Y,),
        out_shape=jax.ShapeDtypeStruct((Y, slots, rows, DH), jnp.bfloat16),
        in_specs=[pl.BlockSpec((1, 1, rows, DH), lambda i: (i, query[1], 0, 0))]
        + [part(near, 0), part(near, 1), part(far, 0), part(far, 1)]
        + [ANY] * (len(extra) + len(after)),
        out_specs=pl.BlockSpec((1, 1, rows, DH), lambda i: (i, slot, 0, 0)),
        input_output_aliases={5: 0} if extra else {},
        compiler_params=params(),
        cost_estimate=COST,
    )(query[0], near[0], near[0], far[0], far[0], *extra, *after)


def frames_body(q_ref, k_ref, v_ref, o_ref):
    frames, _, tokens, _ = q_ref.shape
    size = frames * tokens
    s = scores_of(q_ref[:, 0].reshape(size, DH), k_ref[:, 0].reshape(size, DH))
    row = lax.broadcasted_iota(jnp.int32, (size, size), 0)
    column = lax.broadcasted_iota(jnp.int32, (size, size), 1)
    same = (row & (tokens - 1)) == (column & (tokens - 1))
    s = jnp.where(same, s, -jnp.inf)
    top = s.max(axis=-1, keepdims=True)
    w = jnp.exp2((s - top) * SCALE2)
    total = w.sum(axis=-1, keepdims=True)
    out = jnp.dot(
        w.astype(jnp.bfloat16), v_ref[:, 0].reshape(size, DH), preferred_element_type=jnp.float32
    )
    o_ref[...] = (out / total).astype(jnp.bfloat16).reshape(frames, tokens, DH)


def attend_frames(trio):
    frames, _, rows, _ = trio.shape
    tokens = 32

    def part(n):
        return pl.BlockSpec((frames, 1, tokens, DH), lambda i: (0, n, i, 0))

    return pl.pallas_call(
        frames_body,
        grid=(rows // tokens,),
        out_shape=jax.ShapeDtypeStruct((frames, rows, DH), jnp.bfloat16),
        in_specs=[part(0), part(1), part(2)],
        out_specs=pl.BlockSpec((frames, tokens, DH), lambda i: (0, i, 0)),
        compiler_params=pltpu.CompilerParams(vmem_limit_bytes=VMEM_LIMIT),
        cost_estimate=COST,
    )(trio, trio, trio)


def over(axis, array):
    return lax.cond(
        lax.axis_index("dp") < 8,
        lambda a: lax.all_to_all(a, axis, split_axis=0, concat_axis=0, tiled=True),
        lambda a: a,
        array,
    )


def across(array):
    return lax.ppermute(array, "zh", [(0, 1), (1, 0)])


def on_device(q, k, v):
    rows, width = q.shape[1], q.shape[2]

    (raw,) = pack(
        [(a, j) for j in (0, 1) for a in (k, v)],
        [(Y, 4, rows, DH)],
        [(n, y, 0, (y, n)) for n in range(4) for y in range(Y)],
    )
    far_raw = across(raw)
    more, trio = pack(
        [(a, j) for j in range(CH) for a in (k, v)]
        + [(q, j) for j in range(CH)]
        + [(a, CH + g) for g in range(HT // Y) for a in (q, k, v)],
        [(Y, 12, rows, DH), (HT, 3, rows, DH)],
        [(n, y, 0, (y, n)) for n in range(12) for y in range(Y)]
        + [
            (12 + g * 3 + a, y, 1, (g * Y + y, a))
            for g in range(HT // Y)
            for a in range(3)
            for y in range(Y)
        ],
        (raw,),
    )
    mixed = over("y", more)
    far23 = across(mixed[:, 4:8])
    frames_out = over("tm", attend_frames(over("tm", trio)))
    far01 = over("y", far_raw)
    out = attend((mixed, 8), (mixed, 0), (far01, 0), 2, 0)
    out = over("y", attend((mixed, 9), (mixed, 2), (far01, 2), 2, 1, out))
    early = unpack(
        [out, frames_out],
        [(j, [(0, (y, j)) for y in range(Y)]) for j in range(2)]
        + [(CH + g, [(1, g * Y + y) for y in range(Y)]) for g in range(HT // Y)],
        rows,
        width,
    )
    out = attend((mixed, 10), (mixed, 4), (far23, 0), 2, 0, after=(early,))
    out = over("y", attend((mixed, 11), (mixed, 6), (far23, 2), 2, 1, out))
    return unpack(
        [out], [(2 + j, [(0, (y, j)) for y in range(Y)]) for j in range(2)], rows, width, early
    )


def solution(mesh):
    fine = Mesh(mesh.devices.reshape(8, 8, Y, 2), ("dp", "tm", "y", "zh"))
    spec = P(("dp", "tm"), ("y", "zh"), None)
    return jax.shard_map(
        on_device, mesh=fine, in_specs=(spec, spec, spec), out_specs=spec, check_vma=False
    )
```

time: 242 us -> 182 us (0.75)
  the two profiles are of different devices: /device:TPU:32 before, /device:TPU:4 now
where the time goes in v1:
time: 182 us; the launch traced here: 181 us
  blocking collectives  102 us (56%)
  waiting for transfers between devices  31.1 us (17%)
  Pallas kernels  27.1 us (15%)
  starting transfers between devices  17.9 us (10%)
  local copies, waits for them, and re-layouts  3.26 us (2%)
    all_to_all x6, blocking collectives, over(): lax.all_to_all(a, axis, split_axis=0, concat_axis=0, tiled=True)  102 us
    ppermute x2, waiting for transfers between devices, across(): return lax.ppermute(array, 'zh', [(0, 1), (1, 0)])  31.1 us
    ppermute x2, starting transfers between devices, across(): return lax.ppermute(array, 'zh', [(0, 1), (1, 0)])  17.9 us
    pallas_call x4, Pallas kernels, attend(): pl.pallas_call(attend_body, grid=(Y,), out_shape=jax.ShapeDtypeStruct((Y,...  14.3 us
    pallas_call x2, Pallas kernels, pack(): pl.pallas_call(body, grid=(1,), out_shape=[jax.ShapeDtypeStruct(s, jnp.bf...  5.97 us
    pallas_call x1, Pallas kernels, attend_frames(): pl.pallas_call(frames_body, grid=(rows // tokens,), out_shape=jax.ShapeDt...  4.53 us
  transfers between devices with their start and end apart: 2, of which 1 were waited for; matrix products, arithmetic and copies ran while one was open for 1% of the time, Pallas kernels for 9%

profile of v1, /device:TPU:4, one launch (start us, length us, event | category | flops | bytes accessed | tf_op | source)
XLA Modules:
  0.0 181.2 jit_solution(3437722278723187416)
XLA Ops:
  0.0 2.2 %shard_map.37.refs_18_ = bf16[4,4,192,128]{3,2,1,0:T(8,128)(2,1)} custom-call(bf16[1,192,3072]{2,1,0:T(8,128)(2,1)} %refs_16_.1, bf16[1,192,3072]{2,1,0:T(8,128)(2,1)} %refs_17_.1, bf16[1,192,3072]{2,1,0:T(8,128)(2,1)} %refs_16_.1, bf16[1,192,3072]{2,1,0:T(8,128)(2,1)} %refs_17_.1), custom_call_target="tpu_custom_call" | custom-call | tf_op jit(solution)/shard_map/pallas_call | solution.py:37
  2.2 15.7 %collective-permute-start.1 = (bf16[4,4,192,128]{3,2,1,0:T(8,128)(2,1)}, bf16[4,4,192,128]{3,2,1,0:T(8,128)(2,1)S(1)}, u32[]{:S(2)}, u32[]{:S(2)}) collective-permute-start(bf16[4,4,192,128]{3,2,1,0:T(8,128)(2,1)} %shard_map.37.refs_18_), channel_id=1, source_target_pairs={{0,1},{1,0},{2,3},{3,2},{4,5},{5,4},{6,7},{7,6},{8,9},{9,8},{10,11... | collective-permute-start | bytes 2359304 | tf_op jit(solution)/shard_map/ppermute | solution.py:172
  18.0 3.7 %shard_map.38 = (bf16[4,12,192,128]{3,2,1,0:T(8,128)(2,1)S(1)}, bf16[8,3,192,128]{3,2,1,0:T(8,128)(2,1)}) custom-call(bf16[1,192,3072]{2,1,0:T(8,128)(2,1)} %refs_16_.1, bf16[1,192,3072]{2,1,0:T(8,128)(2,1)} %refs_17_.1, bf16[1,192,3072]{2,1,0:T(8,128)(2,1)} %refs_16_.1, bf16[1,192,3072]{2,1,0:T(8,128)(2,1)} %refs_17_.1, bf16[1,192,3072]{2,1,0:T(8,128)(2,1)} %refs_16_.1, ...), custom_call_target="tpu_custom_call" | custom-call | tf_op jit(solution)/shard_map/pallas_call | solution.py:37
  21.7 33.3 %conditional.6 = (bf16[4,12,192,128]{3,2,1,0:T(8,128)(2,1)S(1)}) conditional(s32[]{:T(128)} %convert_element_type.2, bf16[4,12,192,128]{3,2,1,0:T(8,128)(2,1)S(1)} %get-tuple-element.37, bf16[4,12,192,128]{3,2,1,0:T(8,128)(2,1)S(1)} %get-tuple-element.37), branch_computations={%region_0.0_spmd, %region_1.0_spmd} | conditional | bytes 9437192 | solution.py:163
  21.7 0.2 copy.22
  21.8 33.1 %all_to_all.24 = bf16[4,12,192,128]{3,2,1,0:T(8,128)(2,1)S(1)} all-to-all(bf16[4,12,192,128]{3,2,1,0:T(8,128)(2,1)S(1)} %copy.22), channel_id=1, replica_groups=mesh['dp'=8,'tm'=8,'y'=4,'zh'=2] {'y'}, dimensions={0} | all-to-all | bytes 4718592 | tf_op jit(solution)/shard_map/cond/branch_1_fun/all_to_all | solution.py:165
  55.0 1.0 slice.4
  55.9 2.2 %collective-permute-start = (bf16[4,4,192,128]{3,2,1,0:T(8,128)(2,1)}, bf16[4,4,192,128]{3,2,1,0:T(8,128)(2,1)}, u32[]{:S(2)}, u32[]{:S(2)}) collective-permute-start(bf16[4,4,192,128]{3,2,1,0:T(8,128)(2,1)} %slice.4), channel_id=1, source_target_pairs={{0,1},{1,0},{2,3},{3,2},{4,5},{5,4},{6,7},{7,6},{8,9},{9,8},{10,11... | collective-permute-start | bytes 2359304 | tf_op jit(solution)/shard_map/ppermute | solution.py:172
  58.1 20.8 %conditional.9 = (bf16[8,3,192,128]{3,2,1,0:T(8,128)(2,1)}) conditional(s32[]{:T(128)} %convert_element_type.2, bf16[8,3,192,128]{3,2,1,0:T(8,128)(2,1)} %get-tuple-element.38, bf16[8,3,192,128]{3,2,1,0:T(8,128)(2,1)} %get-tuple-element.38), branch_computations={%region_6.0_spmd, %region_7.0_spmd} | conditional | bytes 7077924 | solution.py:163
  58.1 0.0 copy-start
  58.1 1.3 copy-done
  59.4 19.5 %all_to_all.27 = bf16[8,3,192,128]{3,2,1,0:T(8,128)(2,1)} all-to-all(bf16[8,3,192,128]{3,2,1,0:T(8,128)(2,1)S(1)} %copy-done), channel_id=1, replica_groups=mesh['dp'=8,'tm'=8,'y'=4,'zh'=2] {'tm'}, dimensions={0} | all-to-all | bytes 2359296 | tf_op jit(solution)/shard_map/cond/branch_1_fun/all_to_all | solution.py:165
  78.9 4.5 %shard_map.41 = bf16[8,192,128]{2,1,0:T(8,128)(2,1)S(1)} custom-call(bf16[8,3,192,128]{3,2,1,0:T(8,128)(2,1)} %get-tuple-element.42.q_ref.k_ref.v_ref, bf16[8,3,192,128]{3,2,1,0:T(8,128)(2,1)} %get-tuple-element.42.q_ref.k_ref.v_ref, bf16[8,3,192,128]{3,2,1,0:T(8,128)(2,1)} %get-tuple-element.42.q_ref.k_ref.v_ref), custom_call_target="tpu_custom_call" | custom-call | tf_op jit(solution)/shard_map/pallas_call | solution.py:151
  83.4 11.4 %conditional.10 = (bf16[8,192,128]{2,1,0:T(8,128)(2,1)S(1)}) conditional(s32[]{:T(128)} %convert_element_type.2, bf16[8,192,128]{2,1,0:T(8,128)(2,1)S(1)} %shard_map.41, bf16[8,192,128]{2,1,0:T(8,128)(2,1)S(1)} %shard_map.41), branch_computations={%region_8.0_spmd, %region_9.0_spmd} | conditional | bytes 1572872 | solution.py:163
  83.5 11.3 %all_to_all.28 = bf16[8,192,128]{2,1,0:T(8,128)(2,1)S(1)} all-to-all(bf16[8,192,128]{2,1,0:T(8,128)(2,1)S(1)} %copy.26), channel_id=1, replica_groups=mesh['dp'=8,'tm'=8,'y'=4,'zh'=2] {'tm'}, dimensions={0} | all-to-all | bytes 786432 | tf_op jit(solution)/shard_map/cond/branch_1_fun/all_to_all | solution.py:165
  94.8 0.0 collective-permute-done.1
  94.8 0.7 copy-done.1
  95.6 15.2 %conditional.7 = (bf16[4,4,192,128]{3,2,1,0:T(8,128)(2,1)S(1)}) conditional(s32[]{:T(128)} %convert_element_type.2, bf16[4,4,192,128]{3,2,1,0:T(8,128)(2,1)S(1)} %collective-permute-done.1, bf16[4,4,192,128]{3,2,1,0:T(8,128)(2,1)S(1)} %collective-permute-done.1), branch_computations={%region_2.0_spmd, %region_3.0_spmd} | conditional | bytes 3145736 | solution.py:163
  95.6 0.1 copy.23
  95.6 15.1 %all_to_all.25 = bf16[4,4,192,128]{3,2,1,0:T(8,128)(2,1)S(1)} all-to-all(bf16[4,4,192,128]{3,2,1,0:T(8,128)(2,1)S(1)} %copy.23), channel_id=1, replica_groups=mesh['dp'=8,'tm'=8,'y'=4,'zh'=2] {'y'}, dimensions={0} | all-to-all | bytes 1572864 | tf_op jit(solution)/shard_map/cond/branch_1_fun/all_to_all | solution.py:165
  110.8 3.1 %shard_map.39.rest_0_ = bf16[4,2,192,128]{3,2,1,0:T(8,128)(2,1)S(1)} custom-call(bf16[4,12,192,128]{3,2,1,0:T(8,128)(2,1)S(1)} %get-tuple-element.39.q_ref.kl_ref.vl_ref, bf16[4,12,192,128]{3,2,1,0:T(8,128)(2,1)S(1)} %get-tuple-element.39.q_ref.kl_ref.vl_ref, bf16[4,12,192,128]{3,2,1,0:T(8,128)(2,1)S(1)} %get-tuple-element.39.q_ref.kl_ref.vl_ref, ...), custom_call_target="tpu_custom_call" | custom-call | tf_op jit(solution)/shard_map/pallas_call | solution.py:113
  113.8 3.1 %shard_map.40 = bf16[4,2,192,128]{3,2,1,0:T(8,128)(2,1)S(1)} custom-call(bf16[4,12,192,128]{3,2,1,0:T(8,128)(2,1)S(1)} %get-tuple-element.39.q_ref.kl_ref.vl_ref, bf16[4,12,192,128]{3,2,1,0:T(8,128)(2,1)S(1)} %get-tuple-element.39.q_ref.kl_ref.vl_ref, ...), custom_call_target="tpu_custom_call", output_to_operand_aliasing={{}: (5, {})} | custom-call | tf_op jit(solution)/shard_map/pallas_call | solution.py:113
  116.9 10.3 %conditional.8 = (bf16[4,2,192,128]{3,2,1,0:T(8,128)(2,1)S(1)}) conditional(s32[]{:T(128)} %convert_element_type.2, bf16[4,2,192,128]{3,2,1,0:T(8,128)(2,1)S(1)} %shard_map.40, bf16[4,2,192,128]{3,2,1,0:T(8,128)(2,1)S(1)} %shard_map.40), branch_computations={%region_4.0_spmd, %region_5.0_spmd} | conditional | bytes 1572872 | solution.py:163
  117.0 10.3 %all_to_all.26 = bf16[4,2,192,128]{3,2,1,0:T(8,128)(2,1)S(1)} all-to-all(bf16[4,2,192,128]{3,2,1,0:T(8,128)(2,1)S(1)} %copy.24), channel_id=1, replica_groups=mesh['dp'=8,'tm'=8,'y'=4,'zh'=2] {'y'}, dimensions={0} | all-to-all | bytes 786432 | tf_op jit(solution)/shard_map/cond/branch_1_fun/all_to_all | solution.py:165
  127.2 0.0 copy-done.2
  127.2 1.5 shard_map.42.rest_0_.refs_1_
  128.8 31.1 %collective-permute-done.kr_ref.vr_ref = bf16[4,4,192,128]{3,2,1,0:T(8,128)(2,1)} collective-permute-done((bf16[4,4,192,128]{3,2,1,0:T(8,128)(2,1)}, bf16[4,4,192,128]{3,2,1,0:T(8,128)(2,1)}, u32[]{:S(2)}, u32[]{:S(2)}) %collective-permute-start) | collective-permute-done | bytes 786464 | tf_op jit(solution)/shard_map/ppermute | solution.py:172
  159.9 4.1 %shard_map.43.rest_0_ = bf16[4,2,192,128]{3,2,1,0:T(8,128)(2,1)S(1)} custom-call(bf16[4,12,192,128]{3,2,1,0:T(8,128)(2,1)S(1)} %get-tuple-element.39.q_ref.kl_ref.vl_ref, bf16[4,12,192,128]{3,2,1,0:T(8,128)(2,1)S(1)} %get-tuple-element.39.q_ref.kl_ref.vl_ref, bf16[4,12,192,128]{3,2,1,0:T(8,128)(2,1)S(1)} %get-tuple-element.39.q_ref.kl_ref.vl_ref, ...), custom_call_target="tpu_custom_call" | custom-call | tf_op jit(solution)/shard_map/pallas_call | solution.py:113
  164.0 4.1 %shard_map.44 = bf16[4,2,192,128]{3,2,1,0:T(8,128)(2,1)S(1)} custom-call(bf16[4,12,192,128]{3,2,1,0:T(8,128)(2,1)S(1)} %get-tuple-element.39.q_ref.kl_ref.vl_ref, bf16[4,12,192,128]{3,2,1,0:T(8,128)(2,1)S(1)} %get-tuple-element.39.q_ref.kl_ref.vl_ref, ...), custom_call_target="tpu_custom_call", output_to_operand_aliasing={{}: (5, {})} | custom-call | tf_op jit(solution)/shard_map/pallas_call | solution.py:113
  168.1 12.4 %conditional.11 = (bf16[4,2,192,128]{3,2,1,0:T(8,128)(2,1)S(1)}) conditional(s32[]{:T(128)} %convert_element_type.2, bf16[4,2,192,128]{3,2,1,0:T(8,128)(2,1)S(1)} %shard_map.44, bf16[4,2,192,128]{3,2,1,0:T(8,128)(2,1)S(1)} %shard_map.44), branch_computations={%region_10.0_spmd, %region_11.0_spmd} | conditional | bytes 1572872 | solution.py:163
  168.1 12.3 %all_to_all.29 = bf16[4,2,192,128]{3,2,1,0:T(8,128)(2,1)S(1)} all-to-all(bf16[4,2,192,128]{3,2,1,0:T(8,128)(2,1)S(1)} %copy.27), channel_id=1, replica_groups=mesh['dp'=8,'tm'=8,'y'=4,'zh'=2] {'y'}, dimensions={0} | all-to-all | bytes 786432 | tf_op jit(solution)/shard_map/cond/branch_1_fun/all_to_all | solution.py:165
  180.4 0.8 shard_map.45
  (5 shorter events, 0.1 us)
Async XLA Ops:
  2.2 92.6 %collective-permute-start.1 = (bf16[4,4,192,128]{3,2,1,0:T(8,128)(2,1)}, bf16[4,4,192,128]{3,2,1,0:T(8,128)(2,1)S(1)}, u32[]{:S(2)}, u32[]{:S(2)}) collective-permute-start(bf16[4,4,192,128]{3,2,1,0:T(8,128)(2,1)} %shard_map.37.refs_18_), channel_id=1, source_target_pairs={{0,1},{1,0},{2,3},{3,2},{4,5},{5,4},{6,7},{7,6},{8,9},{9,8},{10,11... | collective-permute-start | bytes 2359304 | tf_op jit(solution)/shard_map/ppermute | solution.py:172
  55.9 103.9 %collective-permute-start = (bf16[4,4,192,128]{3,2,1,0:T(8,128)(2,1)}, bf16[4,4,192,128]{3,2,1,0:T(8,128)(2,1)}, u32[]{:S(2)}, u32[]{:S(2)}) collective-permute-start(bf16[4,4,192,128]{3,2,1,0:T(8,128)(2,1)} %slice.4), channel_id=1, source_target_pairs={{0,1},{1,0},{2,3},{3,2},{4,5},{5,4},{6,7},{7,6},{8,9},{9,8},{10,11... | collective-permute-start | bytes 2359304 | tf_op jit(solution)/shard_map/ppermute | solution.py:172
  58.1 1.3 copy-start
  94.8 0.7 copy-start.1
  116.9 10.3 %copy-start.2 = (bf16[8,192,128]{2,1,0:T(8,128)(2,1)S(1)}, bf16[8,192,128]{2,1,0:T(8,128)(2,1)}, u32[]{:S(2)}) copy-start(bf16[8,192,128]{2,1,0:T(8,128)(2,1)} %copy-done.1) | copy-start | bytes 1179652

commit v2 on v1

v2 whole, which is shorter than its diff:
```python
import math

import jax
import jax.numpy as jnp
from jax import lax
from jax.experimental import pallas as pl
from jax.experimental.pallas import tpu as pltpu
from jax.sharding import Mesh, PartitionSpec as P

HS = 16
HT = 8
DH = 128
Y = 4
SCALE = 1.0 / math.sqrt(DH)
SCALE2 = SCALE * math.log2(math.e)
ANY = pl.BlockSpec(memory_space=pl.ANY)
PARAMS = pltpu.CompilerParams(vmem_limit_bytes=60 * 1024 * 1024)
COST = pl.CostEstimate(flops=0, bytes_accessed=0, transcendentals=0)


def whole(shape):
    return pl.BlockSpec(shape, lambda *_: (0,) * len(shape))


def pack(half, sources, out_shapes, plan, after=()):
    rows, count, skip = sources[0][0].shape[1], len(sources), len(after)

    def body(half_ref, *refs):
        for source, y, o, index in plan:
            refs[count + skip + o][index] = refs[source][0, :, pl.ds(y * DH, DH)]

    def column(group):
        return lambda i, half_ref: (0, 0, group[0] + group[1] * half_ref[0])

    return pl.pallas_call(
        body,
        grid_spec=pltpu.PrefetchScalarGridSpec(
            num_scalar_prefetch=1,
            grid=(1,),
            in_specs=[pl.BlockSpec((1, rows, Y * DH), column(g)) for _, g in sources] + [ANY] * skip,
            out_specs=[whole(s) for s in out_shapes],
        ),
        out_shape=[jax.ShapeDtypeStruct(s, jnp.bfloat16) for s in out_shapes],
        compiler_params=PARAMS,
        cost_estimate=COST,
    )(half, *[array for array, _ in sources], *after)


def unpack(half, pieces, plan, rows, width, base=None):
    count = len(pieces)
    extra = [] if base is None else [base]

    def column(i, half_ref):
        place = jnp.int32(0)
        for n, ((a, b), _) in enumerate(plan):
            place = jnp.where(i == n, a + b * half_ref[0], place)
        return (0, 0, place)

    def body(half_ref, *refs):
        out = refs[count + len(extra)]
        for n, (_, heads) in enumerate(plan):

            @pl.when(pl.program_id(0) == n)
            def _write(heads=heads):
                for y, (p, index) in enumerate(heads):
                    out[0, :, pl.ds(y * DH, DH)] = refs[p][index]

    return pl.pallas_call(
        body,
        grid_spec=pltpu.PrefetchScalarGridSpec(
            num_scalar_prefetch=1,
            grid=(len(plan),),
            in_specs=[whole(p.shape) for p in pieces] + [ANY] * len(extra),
            out_specs=pl.BlockSpec((1, rows, Y * DH), column),
        ),
        out_shape=jax.ShapeDtypeStruct((1, rows, width), jnp.bfloat16),
        input_output_aliases={1 + count: 0} if extra else {},
        compiler_params=PARAMS,
        cost_estimate=COST,
    )(half, *pieces, *extra)


def scores_of(q, k):
    return lax.dot_general(q, k, (((1,), (1,)), ((), ())), preferred_element_type=jnp.float32)


def attend_body(q0_ref, q1_ref, kl_ref, vl_ref, kr_ref, vr_ref, *rest):
    o_ref = rest[-1]
    rows = q0_ref.shape[2]

    def flat(ref):
        return ref[...].reshape(Y * rows, DH)

    q = jnp.where(pl.program_id(0) == 0, q0_ref[0, 0], q1_ref[0, 0])
    sl = scores_of(q, flat(kl_ref))
    sr = scores_of(q, flat(kr_ref))
    top = jnp.maximum(sl.max(axis=-1, keepdims=True), sr.max(axis=-1, keepdims=True))
    wl = jnp.exp2((sl - top) * SCALE2)
    wr = jnp.exp2((sr - top) * SCALE2)
    total = wl.sum(axis=-1, keepdims=True) + wr.sum(axis=-1, keepdims=True)
    out = jnp.dot(wl.astype(jnp.bfloat16), flat(vl_ref), preferred_element_type=jnp.float32)
    out += jnp.dot(wr.astype(jnp.bfloat16), flat(vr_ref), preferred_element_type=jnp.float32)
    o_ref[0, 0] = (out / total).astype(jnp.bfloat16)


def attend(queries, near, far, step, after=()):
    (q0, s0), (q1, s1) = queries
    rows = q0.shape[2]

    def part(slot):
        return pl.BlockSpec((Y, 1, rows, DH), lambda n, i: (0, slot + step * n, 0, 0))

    return pl.pallas_call(
        attend_body,
        grid=(2, Y),
        out_shape=jax.ShapeDtypeStruct((Y, 2, rows, DH), jnp.bfloat16),
        in_specs=[
            pl.BlockSpec((1, 1, rows, DH), lambda n, i: (jnp.where(n == 0, i, Y - 1), s0, 0, 0)),
            pl.BlockSpec((1, 1, rows, DH), lambda n, i: (jnp.where(n == 1, i, 0), s1, 0, 0)),
            part(near[1]),
            part(near[1] + 1),
            part(far[1]),
            part(far[1] + 1),
        ]
        + [ANY] * len(after),
        out_specs=pl.BlockSpec((1, 1, rows, DH), lambda n, i: (i, n, 0, 0)),
        compiler_params=PARAMS,
        cost_estimate=COST,
    )(q0, q1, near[0], near[0], far[0], far[0], *after)


def frames_body(q_ref, k_ref, v_ref, o_ref):
    frames, _, tokens, _ = q_ref.shape
    size = frames * tokens
    s = scores_of(q_ref[:, 0].reshape(size, DH), k_ref[:, 0].reshape(size, DH))
    row = lax.broadcasted_iota(jnp.int32, (size, size), 0)
    column = lax.broadcasted_iota(jnp.int32, (size, size), 1)
    same = (row & (tokens - 1)) == (column & (tokens - 1))
    s = jnp.where(same, s, -jnp.inf)
    top = s.max(axis=-1, keepdims=True)
    w = jnp.exp2((s - top) * SCALE2)
    total = w.sum(axis=-1, keepdims=True)
    out = jnp.dot(
        w.astype(jnp.bfloat16), v_ref[:, 0].reshape(size, DH), preferred_element_type=jnp.float32
    )
    o_ref[...] = (out / total).astype(jnp.bfloat16).reshape(frames, tokens, DH)


def attend_frames(trio):
    frames, _, rows, _ = trio.shape
    tokens = 32

    def part(n):
        return pl.BlockSpec((frames, 1, tokens, DH), lambda i: (0, n, i, 0))

    return pl.pallas_call(
        frames_body,
        grid=(rows // tokens,),
        out_shape=jax.ShapeDtypeStruct((frames, rows, DH), jnp.bfloat16),
        in_specs=[part(0), part(1), part(2)],
        out_specs=pl.BlockSpec((frames, tokens, DH), lambda i: (0, i, 0)),
        compiler_params=PARAMS,
        cost_estimate=COST,
    )(trio, trio, trio)


def over(axis, array):
    return lax.cond(
        lax.axis_index("dp") < 8,
        lambda a: lax.all_to_all(a, axis, split_axis=0, concat_axis=0, tiled=True),
        lambda a: a,
        array,
    )


def across(array):
    return lax.ppermute(array, "zh", [(0, 1), (1, 0)])


def on_device(q, k, v):
    rows, width = q.shape[1], q.shape[2]
    half = lax.axis_index("zh").astype(jnp.int32).reshape(1)
    (raw,) = pack(
        half,
        [(a, (3, -1)) for a in (q, k, v)],
        [(Y, 3, rows, DH)],
        [(n, y, 0, (y, n)) for n in range(3) for y in range(Y)],
    )
    far_raw = across(raw)
    more, trio = pack(
        half,
        [(a, (2, 1)) for a in (q, k, v)]
        + [(a, (j, 0)) for j in range(2) for a in (k, v)]
        + [(q, (j, 0)) for j in range(2)]
        + [(a, (HS // Y + g, 0)) for g in range(HT // Y) for a in (q, k, v)],
        [(Y, 9, rows, DH), (HT, 3, rows, DH)],
        [(n, y, 0, (y, n)) for n in range(9) for y in range(Y)]
        + [
            (9 + g * 3 + a, y, 1, (g * Y + y, a))
            for g in range(HT // Y)
            for a in range(3)
            for y in range(Y)
        ],
        (raw,),
    )
    mixed = over("y", more)
    far_pairs = across(mixed[:, 3:7])
    frames_out = over("tm", attend_frames(over("tm", trio)))
    far = over("y", far_raw)
    own = over("y", attend([(mixed, 0), (far, 0)], (mixed, 1), (far, 1), 0, (frames_out,)))
    back = across(own[:, 1])
    early = unpack(
        half,
        [own, frames_out],
        [((2, 1), [(0, (y, 0)) for y in range(Y)])]
        + [((HS // Y + g, 0), [(1, g * Y + y) for y in range(Y)]) for g in range(HT // Y)],
        rows,
        width,
    )
    pairs = over(
        "y", attend([(mixed, 7), (mixed, 8)], (mixed, 3), (far_pairs, 0), 2, (early,))
    )
    return unpack(
        half,
        [pairs, back],
        [((j, 0), [(0, (y, j)) for y in range(Y)]) for j in range(2)]
        + [((3, -1), [(1, y) for y in range(Y)])],
        rows,
        width,
        early,
    )


def solution(mesh):
    fine = Mesh(mesh.devices.reshape(8, 8, Y, 2), ("dp", "tm", "y", "zh"))
    spec = P(("dp", "tm"), ("y", "zh"), None)
    return jax.shard_map(
        on_device, mesh=fine, in_specs=(spec, spec, spec), out_specs=spec, check_vma=False
    )
```

time: 182 us -> 170 us (0.934)
  the two profiles are of different devices: /device:TPU:4 before, /device:TPU:36 now
where the time goes in v2:
time: 170 us; the launch traced here: 169 us
  blocking collectives  93.2 us (55%)
  starting transfers between devices  29.3 us (17%)
  Pallas kernels  25.6 us (15%)
  waiting for transfers between devices  17.9 us (11%)
  local copies, waits for them, and re-layouts  2.93 us (2%)
    all_to_all x6, blocking collectives, over(): lax.all_to_all(a, axis, split_axis=0, concat_axis=0, tiled=True)  93.2 us
    ppermute x3, starting transfers between devices, across(): return lax.ppermute(array, 'zh', [(0, 1), (1, 0)])  29.3 us
    ppermute x3, waiting for transfers between devices, across(): return lax.ppermute(array, 'zh', [(0, 1), (1, 0)])  17.9 us
    pallas_call x2, Pallas kernels, attend(): pl.pallas_call(attend_body, grid=(2, Y), out_shape=jax.ShapeDtypeStruct((...  13.6 us
    pallas_call x2, Pallas kernels, pack(): pl.pallas_call(body, grid_spec=pltpu.PrefetchScalarGridSpec(num_scalar_pr...  4.46 us
    pallas_call x2, Pallas kernels, unpack(): pl.pallas_call(body, grid_spec=pltpu.PrefetchScalarGridSpec(num_scalar_pr...  3.83 us
    pallas_call x1, Pallas kernels, attend_frames(): pl.pallas_call(frames_body, grid=(rows // tokens,), out_shape=jax.ShapeDt...  3.68 us
  transfers between devices with their start and end apart: 3, of which 1 were waited for; matrix products, arithmetic and copies ran while one was open for 1% of the time, Pallas kernels for 13%

profile of v2, /device:TPU:36, one launch (start us, length us, event | category | flops | bytes accessed | tf_op | source)
XLA Modules:
  0.0 169.1 jit_solution(13946618456716134996)
XLA Ops:
  0.0 2.0 %shard_map.37.refs_15_ = bf16[4,3,192,128]{3,2,1,0:T(8,128)(2,1)} custom-call(s32[1]{0:T(128)} %bitcast.half_ref, bf16[1,192,3072]{2,1,0:T(8,128)(2,1)} %refs_12_.1, bf16[1,192,3072]{2,1,0:T(8,128)(2,1)} %refs_13_.1, bf16[1,192,3072]{2,1,0:T(8,128)(2,1)} %refs_14_.1), custom_call_target="tpu_custom_call" | custom-call | tf_op jit(solution)/shard_map/pallas_call | solution.py:35
  2.0 14.8 %collective-permute-start.1 = (bf16[4,3,192,128]{3,2,1,0:T(8,128)(2,1)}, bf16[4,3,192,128]{3,2,1,0:T(8,128)(2,1)S(1)}, u32[]{:S(2)}, u32[]{:S(2)}) collective-permute-start(bf16[4,3,192,128]{3,2,1,0:T(8,128)(2,1)} %shard_map.37.refs_15_), channel_id=1, source_target_pairs={{0,1},{1,0},{2,3},{3,2},{4,5},{5,4},{6,7},{7,6},{8,9},{9,8},{10,11... | collective-permute-start | bytes 1769480 | tf_op jit(solution)/shard_map/ppermute | solution.py:177
  16.9 2.4 %shard_map.38 = (bf16[4,9,192,128]{3,2,1,0:T(8,128)(2,1)S(1)}, bf16[8,3,192,128]{3,2,1,0:T(8,128)(2,1)S(1)}) custom-call(s32[1]{0:T(128)} %bitcast.half_ref, bf16[1,192,3072]{2,1,0:T(8,128)(2,1)} %refs_12_.1, bf16[1,192,3072]{2,1,0:T(8,128)(2,1)} %refs_13_.1, bf16[1,192,3072]{2,1,0:T(8,128)(2,1)} %refs_14_.1, bf16[1,192,3072]{2,1,0:T(8,128)(2,1)} %refs_13_.1, ...), custom_call_target="tpu_custom_call" | custom-call | tf_op jit(solution)/shard_map/pallas_call | solution.py:35
  19.3 26.9 %conditional.6 = (bf16[4,9,192,128]{3,2,1,0:T(8,128)(2,1)S(1)}) conditional(s32[]{:T(128)} %convert_element_type.2, bf16[4,9,192,128]{3,2,1,0:T(8,128)(2,1)S(1)} %get-tuple-element.37, bf16[4,9,192,128]{3,2,1,0:T(8,128)(2,1)S(1)} %get-tuple-element.37), branch_computations={%region_0.0_spmd, %region_1.0_spmd} | conditional | bytes 7077896 | solution.py:168
  19.3 0.1 copy.20
  19.4 26.8 %all_to_all.24 = bf16[4,9,192,128]{3,2,1,0:T(8,128)(2,1)S(1)} all-to-all(bf16[4,9,192,128]{3,2,1,0:T(8,128)(2,1)S(1)} %copy.20), channel_id=1, replica_groups=mesh['dp'=8,'tm'=8,'y'=4,'zh'=2] {'y'}, dimensions={0} | all-to-all | bytes 3538944 | tf_op jit(solution)/shard_map/cond/branch_1_fun/all_to_all | solution.py:170
  46.2 0.9 slice.8
  47.2 2.2 %collective-permute-start = (bf16[4,4,192,128]{3,2,1,0:T(8,128)(2,1)}, bf16[4,4,192,128]{3,2,1,0:T(8,128)(2,1)}, u32[]{:S(2)}, u32[]{:S(2)}) collective-permute-start(bf16[4,4,192,128]{3,2,1,0:T(8,128)(2,1)} %slice.8), channel_id=1, source_target_pairs={{0,1},{1,0},{2,3},{3,2},{4,5},{5,4},{6,7},{7,6},{8,9},{9,8},{10,11... | collective-permute-start | bytes 2359304 | tf_op jit(solution)/shard_map/ppermute | solution.py:177
  49.4 19.5 %conditional.8 = (bf16[8,3,192,128]{3,2,1,0:T(8,128)(2,1)S(1)}) conditional(s32[]{:T(128)} %convert_element_type.2, bf16[8,3,192,128]{3,2,1,0:T(8,128)(2,1)S(1)} %get-tuple-element.38, bf16[8,3,192,128]{3,2,1,0:T(8,128)(2,1)S(1)} %get-tuple-element.38), branch_computations={%region_4.0_spmd, %region_5.0_spmd} | conditional | bytes 4718600 | solution.py:168
  49.4 0.1 copy.22
  49.5 19.4 %all_to_all.26 = bf16[8,3,192,128]{3,2,1,0:T(8,128)(2,1)S(1)} all-to-all(bf16[8,3,192,128]{3,2,1,0:T(8,128)(2,1)S(1)} %copy.22), channel_id=1, replica_groups=mesh['dp'=8,'tm'=8,'y'=4,'zh'=2] {'tm'}, dimensions={0} | all-to-all | bytes 2359296 | tf_op jit(solution)/shard_map/cond/branch_1_fun/all_to_all | solution.py:170
  68.9 3.7 %shard_map.39 = bf16[8,192,128]{2,1,0:T(8,128)(2,1)} custom-call(bf16[8,3,192,128]{3,2,1,0:T(8,128)(2,1)S(1)} %get-tuple-element.41.q_ref.k_ref.v_ref, bf16[8,3,192,128]{3,2,1,0:T(8,128)(2,1)S(1)} %get-tuple-element.41.q_ref.k_ref.v_ref, bf16[8,3,192,128]{3,2,1,0:T(8,128)(2,1)S(1)} %get-tuple-element.41.q_ref.k_ref.v_ref), custom_call_target="tpu_custom_call" | custom-call | tf_op jit(solution)/shard_map/pallas_call | solution.py:156
  72.5 13.0 %conditional.9 = (bf16[8,192,128]{2,1,0:T(8,128)(2,1)}) conditional(s32[]{:T(128)} %convert_element_type.2, bf16[8,192,128]{2,1,0:T(8,128)(2,1)} %shard_map.39, bf16[8,192,128]{2,1,0:T(8,128)(2,1)} %shard_map.39), branch_computations={%region_6.0_spmd, %region_7.0_spmd} | conditional | bytes 1572872 | solution.py:168
  72.5 1.0 copy.23
  73.5 12.0 %all_to_all.27 = bf16[8,192,128]{2,1,0:T(8,128)(2,1)} all-to-all(bf16[8,192,128]{2,1,0:T(8,128)(2,1)S(1)} %copy.23), channel_id=1, replica_groups=mesh['dp'=8,'tm'=8,'y'=4,'zh'=2] {'tm'}, dimensions={0} | all-to-all | bytes 786432 | tf_op jit(solution)/shard_map/cond/branch_1_fun/all_to_all | solution.py:170
  85.6 0.0 copy-start
  85.6 17.9 %collective-permute-done.1 = bf16[4,3,192,128]{3,2,1,0:T(8,128)(2,1)S(1)} collective-permute-done((bf16[4,3,192,128]{3,2,1,0:T(8,128)(2,1)}, bf16[4,3,192,128]{3,2,1,0:T(8,128)(2,1)S(1)}, u32[]{:S(2)}, u32[]{:S(2)}) %collective-permute-start.1) | collective-permute-done | bytes 589856 | tf_op jit(solution)/shard_map/ppermute | solution.py:177
  103.4 12.7 %conditional.7 = (bf16[4,3,192,128]{3,2,1,0:T(8,128)(2,1)S(1)}) conditional(s32[]{:T(128)} %convert_element_type.2, bf16[4,3,192,128]{3,2,1,0:T(8,128)(2,1)S(1)} %collective-permute-done.1, bf16[4,3,192,128]{3,2,1,0:T(8,128)(2,1)S(1)} %collective-permute-done.1), branch_computations={%region_2.0_spmd, %region_3.0_spmd} | conditional | bytes 2359304 | solution.py:168
  103.5 12.7 %all_to_all.25 = bf16[4,3,192,128]{3,2,1,0:T(8,128)(2,1)S(1)} all-to-all(bf16[4,3,192,128]{3,2,1,0:T(8,128)(2,1)S(1)} %copy.21), channel_id=1, replica_groups=mesh['dp'=8,'tm'=8,'y'=4,'zh'=2] {'y'}, dimensions={0} | all-to-all | bytes 1179648 | tf_op jit(solution)/shard_map/cond/branch_1_fun/all_to_all | solution.py:170
  116.2 0.0 copy-done
  116.2 6.1 %shard_map.40 = bf16[4,2,192,128]{3,2,1,0:T(8,128)(2,1)S(1)} custom-call(bf16[4,9,192,128]{3,2,1,0:T(8,128)(2,1)S(1)} %get-tuple-element.39.q0_ref.kl_ref.vl_ref.q1_ref, bf16[4,3,192,128]{3,2,1,0:T(8,128)(2,1)S(1)} %get-tuple-element.40.q1_ref.kr_ref.vr_ref, bf16[4,9,192,128]{3,2,1,0:T(8,128)(2,1)S(1)} %get-tuple-element.39.q0_ref.kl_ref.vl_ref.q1_ref, ...), custom_call_target="tpu_custom_call" | custom-call | tf_op jit(solution)/shard_map/pallas_call | solution.py:113
  122.3 9.8 %conditional.10 = (bf16[4,2,192,128]{3,2,1,0:T(8,128)(2,1)S(1)}) conditional(s32[]{:T(128)} %convert_element_type.2, bf16[4,2,192,128]{3,2,1,0:T(8,128)(2,1)S(1)} %shard_map.40, bf16[4,2,192,128]{3,2,1,0:T(8,128)(2,1)S(1)} %shard_map.40), branch_computations={%region_8.0_spmd, %region_9.0_spmd} | conditional | bytes 1572872 | solution.py:168
  122.3 9.8 %all_to_all.28 = bf16[4,2,192,128]{3,2,1,0:T(8,128)(2,1)S(1)} all-to-all(bf16[4,2,192,128]{3,2,1,0:T(8,128)(2,1)S(1)} %copy.24), channel_id=1, replica_groups=mesh['dp'=8,'tm'=8,'y'=4,'zh'=2] {'y'}, dimensions={0} | all-to-all | bytes 786432 | tf_op jit(solution)/shard_map/cond/branch_1_fun/all_to_all | solution.py:170
  132.1 12.3 %collective-permute-start.2 = (bf16[4,192,128]{2,1,0:T(8,128)(2,1)S(1)}, bf16[4,192,128]{2,1,0:T(8,128)(2,1)S(1)}, u32[]{:S(2)}, u32[]{:S(2)}) collective-permute-start(bf16[4,192,128]{2,1,0:T(8,128)(2,1)S(1)} %slice_bitcast_fusion), channel_id=1, source_target_pairs={{0,1},{1,0},{2,3},{3,2},{4,5},{5,4},{6,7},{7,6},{8,9},{9,8},{10,11... | collective-permute-start | bytes 589832 | tf_op jit(solution)/shard_map/ppermute | solution.py:177
  144.5 1.5 shard_map.41.rest_0_.refs_2_
  145.9 0.0 collective-permute-done.kr_ref.vr_ref
  145.9 7.6 %shard_map.42 = bf16[4,2,192,128]{3,2,1,0:T(8,128)(2,1)S(1)} custom-call(bf16[4,9,192,128]{3,2,1,0:T(8,128)(2,1)S(1)} %get-tuple-element.39.q0_ref.kl_ref.vl_ref.q1_ref, bf16[4,9,192,128]{3,2,1,0:T(8,128)(2,1)S(1)} %get-tuple-element.39.q0_ref.kl_ref.vl_ref.q1_ref, bf16[4,9,192,128]{3,2,1,0:T(8,128)(2,1)S(1)} %get-tuple-element.39.q0_ref.kl_ref.vl_ref.q1_ref, ...), custom_call_target="tpu_custom_call" | custom-call | tf_op jit(solution)/shard_map/pallas_call | solution.py:113
  153.5 12.6 %conditional.11 = (bf16[4,2,192,128]{3,2,1,0:T(8,128)(2,1)S(1)}) conditional(s32[]{:T(128)} %convert_element_type.2, bf16[4,2,192,128]{3,2,1,0:T(8,128)(2,1)S(1)} %shard_map.42, bf16[4,2,192,128]{3,2,1,0:T(8,128)(2,1)S(1)} %shard_map.42), branch_computations={%region_10.0_spmd, %region_11.0_spmd} | conditional | bytes 1572872 | solution.py:168
  153.6 12.5 %all_to_all.29 = bf16[4,2,192,128]{3,2,1,0:T(8,128)(2,1)S(1)} all-to-all(bf16[4,2,192,128]{3,2,1,0:T(8,128)(2,1)S(1)} %copy.25), channel_id=1, replica_groups=mesh['dp'=8,'tm'=8,'y'=4,'zh'=2] {'y'}, dimensions={0} | all-to-all | bytes 786432 | tf_op jit(solution)/shard_map/cond/branch_1_fun/all_to_all | solution.py:170
  166.1 0.0 collective-permute-done.2.refs_1_
  166.1 0.7 copy-done.1
  166.8 2.4 %shard_map.43 = bf16[1,192,3072]{2,1,0:T(8,128)(2,1)} custom-call(s32[1]{0:T(128)} %bitcast.half_ref, bf16[4,2,192,128]{3,2,1,0:T(8,128)(2,1)S(1)} %get-tuple-element.44.refs_0_, bf16[4,192,128]{2,1,0:T(8,128)(2,1)} %copy-done.1, bf16[1,192,3072]{2,1,0:T(8,128)(2,1)} %shard_map.41.rest_0_.refs_2_), custom_call_target="tpu_custom_call", output_to_operand_aliasing={{}: (3, {})} | custom-call | tf_op jit(solution)/shard_map/pallas_call | solution.py:68
  (5 shorter events, 0.1 us)
Async XLA Ops:
  2.0 101.4 %collective-permute-start.1 = (bf16[4,3,192,128]{3,2,1,0:T(8,128)(2,1)}, bf16[4,3,192,128]{3,2,1,0:T(8,128)(2,1)S(1)}, u32[]{:S(2)}, u32[]{:S(2)}) collective-permute-start(bf16[4,3,192,128]{3,2,1,0:T(8,128)(2,1)} %shard_map.37.refs_15_), channel_id=1, source_target_pairs={{0,1},{1,0},{2,3},{3,2},{4,5},{5,4},{6,7},{7,6},{8,9},{9,8},{10,11... | collective-permute-start | bytes 1769480 | tf_op jit(solution)/shard_map/ppermute | solution.py:177
  47.2 98.8 %collective-permute-start = (bf16[4,4,192,128]{3,2,1,0:T(8,128)(2,1)}, bf16[4,4,192,128]{3,2,1,0:T(8,128)(2,1)}, u32[]{:S(2)}, u32[]{:S(2)}) collective-permute-start(bf16[4,4,192,128]{3,2,1,0:T(8,128)(2,1)} %slice.8), channel_id=1, source_target_pairs={{0,1},{1,0},{2,3},{3,2},{4,5},{5,4},{6,7},{7,6},{8,9},{9,8},{10,11... | collective-permute-start | bytes 2359304 | tf_op jit(solution)/shard_map/ppermute | solution.py:177
  85.6 30.6 %copy-start = (bf16[8,192,128]{2,1,0:T(8,128)(2,1)S(1)}, bf16[8,192,128]{2,1,0:T(8,128)(2,1)}, u32[]{:S(2)}) copy-start(bf16[8,192,128]{2,1,0:T(8,128)(2,1)} %get-tuple-element.42.rest_0_.refs_1_) | copy-start | bytes 1179652
  132.1 34.0 %collective-permute-start.2 = (bf16[4,192,128]{2,1,0:T(8,128)(2,1)S(1)}, bf16[4,192,128]{2,1,0:T(8,128)(2,1)S(1)}, u32[]{:S(2)}, u32[]{:S(2)}) collective-permute-start(bf16[4,192,128]{2,1,0:T(8,128)(2,1)S(1)} %slice_bitcast_fusion), channel_id=1, source_target_pairs={{0,1},{1,0},{2,3},{3,2},{4,5},{5,4},{6,7},{7,6},{8,9},{9,8},{10,11... | collective-permute-start | bytes 589832 | tf_op jit(solution)/shard_map/ppermute | solution.py:177
  166.1 0.7 copy-start.1

commit v3 on v2

v3 whole, which is shorter than its diff:
```python
import functools
import math

import jax
import jax.numpy as jnp
from jax import lax
from jax.experimental import pallas as pl
from jax.experimental.pallas import tpu as pltpu
from jax.sharding import Mesh, PartitionSpec as P

HS = 16
HT = 8
DH = 128
Y = 4
SCALE = 1.0 / math.sqrt(DH)
SCALE2 = SCALE * math.log2(math.e)
ANY = pl.BlockSpec(memory_space=pl.ANY)
PARAMS = pltpu.CompilerParams(vmem_limit_bytes=66_900_000)
SMALL = pltpu.CompilerParams(vmem_limit_bytes=60 * 1024 * 1024)
COST = pl.CostEstimate(flops=0, bytes_accessed=0, transcendentals=0)


def whole(shape):
    return pl.BlockSpec(shape, lambda *_: (0,) * len(shape))


def pack(half, sources, out_shapes, plan, after=()):
    rows, count, skip = sources[0][0].shape[1], len(sources), len(after)

    def body(half_ref, *refs):
        for source, y, o, index in plan:
            refs[count + skip + o][index] = refs[source][0, :, pl.ds(y * DH, DH)]

    def column(group):
        return lambda i, half_ref: (0, 0, group[0] + group[1] * half_ref[0])

    return pl.pallas_call(
        body,
        grid_spec=pltpu.PrefetchScalarGridSpec(
            num_scalar_prefetch=1,
            grid=(1,),
            in_specs=[pl.BlockSpec((1, rows, Y * DH), column(g)) for _, g in sources] + [ANY] * skip,
            out_specs=[whole(s) for s in out_shapes],
        ),
        out_shape=[jax.ShapeDtypeStruct(s, jnp.bfloat16) for s in out_shapes],
        compiler_params=PARAMS,
        cost_estimate=COST,
    )(half, *[array for array, _ in sources], *after)


def here(ref):
    if isinstance(ref, tuple):
        return jnp.where(lax.axis_index("zh") == 0, ref[0], ref[1])
    return ref


def unpack(pieces, plan, first, rows, width, base=None):
    count = len(pieces)
    extra = [] if base is None else [base]

    def body(*refs):
        out = refs[count + len(extra)]
        for n, place in enumerate(plan):
            if isinstance(place[0], tuple):
                head = here(tuple(refs[p][index] for p, index in place))
            else:
                head = refs[place[0]][place[1]]
            out[0, :, pl.ds(n * DH, DH)] = head

    return pl.pallas_call(
        body,
        grid=(1,),
        out_shape=jax.ShapeDtypeStruct((1, rows, width), jnp.bfloat16),
        in_specs=[whole(p.shape) for p in pieces] + [ANY] * len(extra),
        out_specs=pl.BlockSpec((1, rows, len(plan) * DH), lambda i: (0, 0, first // len(plan))),
        input_output_aliases={count: 0} if extra else {},
        compiler_params=PARAMS,
        cost_estimate=COST,
    )(*pieces, *extra)


def scores_of(q, k):
    return lax.dot_general(q, k, (((1,), (1,)), ((), ())), preferred_element_type=jnp.float32)


def attend_body(jobs, *refs):
    o_ref = refs[-1]
    _, _, rows, _ = o_ref.shape
    size, parts = Y * rows, 2
    step = size // parts

    def flat(n):
        return refs[n][...].reshape(size, DH)

    def scores(task):
        q, kl, _, kr, _ = jobs[task // parts]
        query = flat(q)[task % parts * step : (task % parts + 1) * step]
        return scores_of(query, flat(kl)), scores_of(query, flat(kr))

    def weigh(w, n):
        both = jnp.concatenate([flat(n), jnp.ones((size, DH), jnp.bfloat16)], axis=-1)
        return jnp.dot(w.astype(jnp.bfloat16), both, preferred_element_type=jnp.float32)

    tasks = len(jobs) * parts
    ahead, outs = scores(0), []
    for task in range(tasks):
        (sl, sr), ahead = ahead, scores(task + 1) if task + 1 < tasks else None
        top = jnp.maximum(sl.max(axis=-1, keepdims=True), sr.max(axis=-1, keepdims=True))
        _, _, vl, _, vr = jobs[task // parts]
        out = weigh(jnp.exp2((sl - top) * SCALE2), vl) + weigh(jnp.exp2((sr - top) * SCALE2), vr)
        outs.append((out[:, :DH] / out[:, DH:]).astype(jnp.bfloat16))
    for n in range(len(jobs)):
        o_ref[:, n] = jnp.concatenate(outs[n * parts : (n + 1) * parts]).reshape(Y, rows, DH)


def attend(jobs, slots, slot=0, base=None, after=(), limit=PARAMS):
    operands, indices = [], []

    def use(array, n):
        for m, (other, k) in enumerate(operands):
            if other is array and k == n:
                return m
        operands.append((array, n))
        return len(operands) - 1

    for (q, sq), (near, sn), (far, sf) in jobs:
        indices.append((use(q, sq), use(near, sn), use(near, sn + 1), use(far, sf), use(far, sf + 1)))
    rows = jobs[0][0][0].shape[2]
    extra = [] if base is None else [base]
    return pl.pallas_call(
        functools.partial(attend_body, indices),
        grid=(1,),
        out_shape=jax.ShapeDtypeStruct((Y, slots, rows, DH), jnp.bfloat16),
        in_specs=[
            pl.BlockSpec((Y, 1, rows, DH), lambda i, n=n: (0, n, 0, 0)) for _, n in operands
        ]
        + [ANY] * (len(extra) + len(after)),
        out_specs=pl.BlockSpec(
            (Y, len(jobs), rows, DH), lambda i: (0, slot // len(jobs), 0, 0)
        ),
        input_output_aliases={len(operands): 0} if extra else {},
        compiler_params=limit,
        cost_estimate=COST,
    )(*[array for array, _ in operands], *extra, *after)


def take(array, first, count, after=()):
    _, _, rows, _ = array.shape

    def body(i_ref, *refs):
        refs[-1][...] = i_ref[...]

    return pl.pallas_call(
        body,
        grid=(Y,),
        out_shape=jax.ShapeDtypeStruct((Y, count, rows, DH), jnp.bfloat16),
        in_specs=[pl.BlockSpec((1, count, rows, DH), lambda i: (i, first // count, 0, 0))]
        + [ANY] * len(after),
        out_specs=pl.BlockSpec((1, count, rows, DH), lambda i: (i, 0, 0, 0)),
        compiler_params=PARAMS,
        cost_estimate=COST,
    )(array, *after)


def frames_body(q_ref, k_ref, v_ref, o_ref):
    frames, _, tokens, _ = q_ref.shape
    size = frames * tokens
    s = scores_of(q_ref[:, 0].reshape(size, DH), k_ref[:, 0].reshape(size, DH))
    row = lax.broadcasted_iota(jnp.int32, (size, size), 0)
    column = lax.broadcasted_iota(jnp.int32, (size, size), 1)
    same = (row & (tokens - 1)) == (column & (tokens - 1))
    s = jnp.where(same, s, -jnp.inf)
    top = s.max(axis=-1, keepdims=True)
    w = jnp.exp2((s - top) * SCALE2)
    total = w.sum(axis=-1, keepdims=True)
    out = jnp.dot(
        w.astype(jnp.bfloat16), v_ref[:, 0].reshape(size, DH), preferred_element_type=jnp.float32
    )
    o_ref[...] = (out / total).astype(jnp.bfloat16).reshape(frames, tokens, DH)


def attend_frames(trio):
    frames, _, rows, _ = trio.shape
    tokens = 32

    def part(n):
        return pl.BlockSpec((frames, 1, tokens, DH), lambda i: (0, n, i, 0))

    return pl.pallas_call(
        frames_body,
        grid=(rows // tokens,),
        out_shape=jax.ShapeDtypeStruct((frames, rows, DH), jnp.bfloat16),
        in_specs=[part(0), part(1), part(2)],
        out_specs=pl.BlockSpec((frames, tokens, DH), lambda i: (0, i, 0)),
        compiler_params=PARAMS,
        cost_estimate=COST,
    )(trio, trio, trio)


def over(axis, array):
    return lax.cond(
        lax.axis_index("dp") < 8,
        lambda a: lax.all_to_all(a, axis, split_axis=0, concat_axis=0, tiled=True),
        jnp.zeros_like,
        array,
    )


def across(array):
    return lax.ppermute(array, "zh", [(0, 1), (1, 0)])


def on_device(q, k, v):
    rows, width = q.shape[1], q.shape[2]
    half = lax.axis_index("zh").astype(jnp.int32).reshape(1)
    (raw,) = pack(
        half,
        [(a, (3, -1)) for a in (q, k, v)],
        [(Y, 3, rows, DH)],
        [(n, y, 0, (y, n)) for n in range(3) for y in range(Y)],
    )
    far_raw = across(raw)
    more, trio = pack(
        half,
        [(a, (j, 0)) for j in range(2) for a in (k, v)]
        + [(q, (j, 0)) for j in range(2)]
        + [(a, (2, 1)) for a in (q, k, v)]
        + [(a, (HS // Y + g, 0)) for g in range(HT // Y) for a in (q, k, v)],
        [(Y, 9, rows, DH), (HT, 3, rows, DH)],
        [(n, y, 0, (y, n)) for n in range(9) for y in range(Y)]
        + [
            (9 + g * 3 + a, y, 1, (g * Y + y, a))
            for g in range(HT // Y)
            for a in range(3)
            for y in range(Y)
        ],
        (raw,),
    )
    mixed = over("y", more)
    far01 = across(take(mixed, 0, 4))
    frames_out = over("tm", attend_frames(over("tm", trio)))
    early = unpack([frames_out], [(0, h) for h in range(HT)], HS, rows, width)
    far = over("y", far_raw)
    own = over(
        "y",
        attend(
            [((mixed, 6), (mixed, 7), (far, 1)), ((far, 0), (mixed, 7), (far, 1))], 2, after=(early,), limit=SMALL
        ),
    )
    back = across(own[:, 1])
    jobs = [((mixed, 4 + j), (mixed, 2 * j), (far01, 2 * j)) for j in range(2)]
    pairs = over("y", attend(jobs, 2, after=(own,), limit=SMALL))
    return unpack(
        [pairs, own, back],
        [(0, (y, j)) for j in range(2) for y in range(Y)]
        + [((1, (y, 0)), (2, y)) for y in range(Y)]
        + [((2, y), (1, (y, 0))) for y in range(Y)],
        0,
        rows,
        width,
        early,
    )


def solution(mesh):
    fine = Mesh(mesh.devices.reshape(8, 8, Y, 2), ("dp", "tm", "y", "zh"))
    spec = P(("dp", "tm"), ("y", "zh"), None)
    return jax.shard_map(
        on_device, mesh=fine, in_specs=(spec, spec, spec), out_specs=spec, check_vma=False
    )
```

time: 170 us -> 166 us (0.976)
  the two profiles are of different devices: /device:TPU:36 before, /device:TPU:1 now
where the time goes in v3:
time: 166 us; the launch traced here: 165 us
  blocking collectives  104 us (63%)
  starting transfers between devices  30.8 us (19%)
  Pallas kernels  27.2 us (16%)
  waiting for transfers between devices  3.4 us (2%)
    all_to_all x6, blocking collectives, over(): lax.all_to_all(a, axis, split_axis=0, concat_axis=0, tiled=True)  104 us
    ppermute x3, starting transfers between devices, across(): return lax.ppermute(array, 'zh', [(0, 1), (1, 0)])  30.8 us
    pallas_call x2, Pallas kernels, attend(): pl.pallas_call(functools.partial(attend_body, indices), grid=(1,), out_sh...  8.5 us
    pallas_call x2, Pallas kernels, pack(): pl.pallas_call(body, grid_spec=pltpu.PrefetchScalarGridSpec(num_scalar_pr...  6.05 us
    pallas_call x1, Pallas kernels, attend_frames(): pl.pallas_call(frames_body, grid=(rows // tokens,), out_shape=jax.ShapeDt...  5.32 us
    pallas_call x2, Pallas kernels, unpack(): pl.pallas_call(body, grid=(1,), out_shape=jax.ShapeDtypeStruct((1, rows,...  4.08 us
    ppermute x3, waiting for transfers between devices, across(): return lax.ppermute(array, 'zh', [(0, 1), (1, 0)])  3.4 us
  transfers between devices with their start and end apart: 3, of which 1 were waited for; matrix products, arithmetic and copies ran while one was open for 0% of the time, Pallas kernels for 14%

profile of v3, /device:TPU:1, one launch (start us, length us, event | category | flops | bytes accessed | tf_op | source)
XLA Modules:
  0.0 165.2 jit_solution(10856230435553417019)
XLA Ops:
  0.0 2.0 %shard_map.37.refs_15_ = bf16[4,3,192,128]{3,2,1,0:T(8,128)(2,1)} custom-call(s32[1]{0:T(128)} %bitcast.half_ref, bf16[1,192,3072]{2,1,0:T(8,128)(2,1)} %refs_12_.1, bf16[1,192,3072]{2,1,0:T(8,128)(2,1)} %refs_13_.1, bf16[1,192,3072]{2,1,0:T(8,128)(2,1)} %refs_14_.1), custom_call_target="tpu_custom_call" | custom-call | tf_op jit(solution)/shard_map/pallas_call | solution.py:37
  2.0 16.3 %collective-permute-start.1 = (bf16[4,3,192,128]{3,2,1,0:T(8,128)(2,1)}, bf16[4,3,192,128]{3,2,1,0:T(8,128)(2,1)}, u32[]{:S(2)}, u32[]{:S(2)}) collective-permute-start(bf16[4,3,192,128]{3,2,1,0:T(8,128)(2,1)} %shard_map.37.refs_15_), channel_id=1, source_target_pairs={{0,1},{1,0},{2,3},{3,2},{4,5},{5,4},{6,7},{7,6},{8,9},{9,8},{10,11... | collective-permute-start | bytes 1769480 | tf_op jit(solution)/shard_map/ppermute | solution.py:210
  18.3 4.0 %shard_map.38 = (bf16[4,9,192,128]{3,2,1,0:T(8,128)(2,1)}, bf16[8,3,192,128]{3,2,1,0:T(8,128)(2,1)}) custom-call(s32[1]{0:T(128)} %bitcast.half_ref, bf16[1,192,3072]{2,1,0:T(8,128)(2,1)} %refs_13_.1, bf16[1,192,3072]{2,1,0:T(8,128)(2,1)} %refs_14_.1, bf16[1,192,3072]{2,1,0:T(8,128)(2,1)} %refs_13_.1, bf16[1,192,3072]{2,1,0:T(8,128)(2,1)} %refs_14_.1, ...), custom_call_target="tpu_custom_call" | custom-call | tf_op jit(solution)/shard_map/pallas_call | solution.py:37
  22.3 25.9 %conditional.6 = (bf16[4,9,192,128]{3,2,1,0:T(8,128)(2,1)}) conditional(s32[]{:T(128)} %convert_element_type.2, () %tuple.42, bf16[4,9,192,128]{3,2,1,0:T(8,128)(2,1)} %get-tuple-element.31), branch_computations={%region_0.0_spmd, %region_1.0_spmd} | conditional | bytes 3538952 | solution.py:201
  22.3 25.9 %all_to_all.24 = bf16[4,9,192,128]{3,2,1,0:T(8,128)(2,1)} all-to-all(bf16[4,9,192,128]{3,2,1,0:T(8,128)(2,1)} %param.1), channel_id=1, replica_groups=mesh['dp'=8,'tm'=8,'y'=4,'zh'=2] {'y'}, dimensions={0} | all-to-all | bytes 3538944 | tf_op jit(solution)/shard_map/cond/branch_1_fun/all_to_all | solution.py:203
  48.2 3.3 %shard_map.39 = bf16[4,4,192,128]{3,2,1,0:T(8,128)(2,1)} custom-call(bf16[4,9,192,128]{3,2,1,0:T(8,128)(2,1)} %get-tuple-element.33.i_ref.refs_0_.refs_1_.refs_2_.refs_5_.refs_6_.refs_7_), custom_call_target="tpu_custom_call" | custom-call | tf_op jit(solution)/shard_map/pallas_call | solution.py:153
  51.5 1.9 %collective-permute-start = (bf16[4,4,192,128]{3,2,1,0:T(8,128)(2,1)}, bf16[4,4,192,128]{3,2,1,0:T(8,128)(2,1)}, u32[]{:S(2)}, u32[]{:S(2)}) collective-permute-start(bf16[4,4,192,128]{3,2,1,0:T(8,128)(2,1)} %shard_map.39), channel_id=1, source_target_pairs={{0,1},{1,0},{2,3},{3,2},{4,5},{5,4},{6,7},{7,6},{8,9},{9,8},{10,11... | collective-permute-start | bytes 2359304 | tf_op jit(solution)/shard_map/ppermute | solution.py:210
  53.4 23.6 %conditional.8 = (bf16[8,3,192,128]{3,2,1,0:T(8,128)(2,1)}) conditional(s32[]{:T(128)} %convert_element_type.2, () %tuple.46, bf16[8,3,192,128]{3,2,1,0:T(8,128)(2,1)} %get-tuple-element.32), branch_computations={%region_4.0_spmd, %region_5.0_spmd} | conditional | bytes 2359304 | solution.py:201
  53.4 23.6 %all_to_all.26 = bf16[8,3,192,128]{3,2,1,0:T(8,128)(2,1)} all-to-all(bf16[8,3,192,128]{3,2,1,0:T(8,128)(2,1)} %param.5), channel_id=1, replica_groups=mesh['dp'=8,'tm'=8,'y'=4,'zh'=2] {'tm'}, dimensions={0} | all-to-all | bytes 2359296 | tf_op jit(solution)/shard_map/cond/branch_1_fun/all_to_all | solution.py:203
  77.0 5.3 %shard_map.40 = bf16[8,192,128]{2,1,0:T(8,128)(2,1)} custom-call(bf16[8,3,192,128]{3,2,1,0:T(8,128)(2,1)} %get-tuple-element.35.q_ref.k_ref.v_ref, bf16[8,3,192,128]{3,2,1,0:T(8,128)(2,1)} %get-tuple-element.35.q_ref.k_ref.v_ref, bf16[8,3,192,128]{3,2,1,0:T(8,128)(2,1)} %get-tuple-element.35.q_ref.k_ref.v_ref), custom_call_target="tpu_custom_call" | custom-call | tf_op jit(solution)/shard_map/pallas_call | solution.py:189
  82.3 13.0 %conditional.9 = (bf16[8,192,128]{2,1,0:T(8,128)(2,1)}) conditional(s32[]{:T(128)} %convert_element_type.2, () %tuple.45, bf16[8,192,128]{2,1,0:T(8,128)(2,1)} %shard_map.40), branch_computations={%region_6.0_spmd, %region_7.0_spmd} | conditional | bytes 786440 | solution.py:201
  82.3 13.0 %all_to_all.27 = bf16[8,192,128]{2,1,0:T(8,128)(2,1)} all-to-all(bf16[8,192,128]{2,1,0:T(8,128)(2,1)} %param.7), channel_id=1, replica_groups=mesh['dp'=8,'tm'=8,'y'=4,'zh'=2] {'tm'}, dimensions={0} | all-to-all | bytes 786432 | tf_op jit(solution)/shard_map/cond/branch_1_fun/all_to_all | solution.py:203
  95.4 1.9 %shard_map.41.refs_6_.refs_3_ = bf16[1,192,3072]{2,1,0:T(8,128)(2,1)} custom-call(bf16[8,192,128]{2,1,0:T(8,128)(2,1)} %get-tuple-element.36.refs_0_), custom_call_target="tpu_custom_call" | custom-call | tf_op jit(solution)/shard_map/pallas_call | solution.py:70
  97.2 0.0 collective-permute-done.1
  97.2 12.8 %conditional.7 = (bf16[4,3,192,128]{3,2,1,0:T(8,128)(2,1)S(1)}) conditional(s32[]{:T(128)} %convert_element_type.2, () %tuple.44, bf16[4,3,192,128]{3,2,1,0:T(8,128)(2,1)} %collective-permute-done.1), branch_computations={%region_2.0_spmd, %region_3.0_spmd} | conditional | bytes 1179656 | solution.py:201
  97.2 12.8 %all_to_all.25 = bf16[4,3,192,128]{3,2,1,0:T(8,128)(2,1)S(1)} all-to-all(bf16[4,3,192,128]{3,2,1,0:T(8,128)(2,1)} %param.3), channel_id=1, replica_groups=mesh['dp'=8,'tm'=8,'y'=4,'zh'=2] {'y'}, dimensions={0} | all-to-all | bytes 1179648 | tf_op jit(solution)/shard_map/cond/branch_1_fun/all_to_all | solution.py:203
  110.0 4.0 %shard_map.42 = bf16[4,2,192,128]{3,2,1,0:T(8,128)(2,1)S(1)} custom-call(bf16[4,9,192,128]{3,2,1,0:T(8,128)(2,1)} %get-tuple-element.33.i_ref.refs_0_.refs_1_.refs_2_.refs_5_.refs_6_.refs_7_, bf16[4,9,192,128]{3,2,1,0:T(8,128)(2,1)} %get-tuple-element.33.i_ref.refs_0_.refs_1_.refs_2_.refs_5_.refs_6_.refs_7_, ...), custom_call_target="tpu_custom_call" | custom-call | tf_op jit(solution)/shard_map/pallas_call | solution.py:130
  114.0 9.0 %conditional.10 = (bf16[4,2,192,128]{3,2,1,0:T(8,128)(2,1)S(1)}) conditional(s32[]{:T(128)} %convert_element_type.2, () %tuple.43, bf16[4,2,192,128]{3,2,1,0:T(8,128)(2,1)S(1)} %shard_map.42), branch_computations={%region_8.0_spmd, %region_9.0_spmd} | conditional | bytes 786440 | solution.py:201
  114.0 9.0 %all_to_all.28 = bf16[4,2,192,128]{3,2,1,0:T(8,128)(2,1)S(1)} all-to-all(bf16[4,2,192,128]{3,2,1,0:T(8,128)(2,1)S(1)} %param.9), channel_id=1, replica_groups=mesh['dp'=8,'tm'=8,'y'=4,'zh'=2] {'y'}, dimensions={0} | all-to-all | bytes 786432 | tf_op jit(solution)/shard_map/cond/branch_1_fun/all_to_all | solution.py:203
  123.1 0.0 copy-start
  123.1 12.7 %collective-permute-start.2 = (bf16[4,192,128]{2,1,0:T(8,128)(2,1)S(1)}, bf16[4,192,128]{2,1,0:T(8,128)(2,1)}, u32[]{:S(2)}, u32[]{:S(2)}) collective-permute-start(bf16[4,192,128]{2,1,0:T(8,128)(2,1)S(1)} %slice_bitcast_fusion), channel_id=1, source_target_pairs={{0,1},{1,0},{2,3},{3,2},{4,5},{5,4},{6,7},{7,6},{8,9},{9,8},{10,11... | collective-permute-start | bytes 589832 | tf_op jit(solution)/shard_map/ppermute | solution.py:210
  135.8 0.0 collective-permute-done.refs_3_.refs_4_.refs_8_.refs_9_
  135.8 4.5 %shard_map.43 = bf16[4,2,192,128]{3,2,1,0:T(8,128)(2,1)S(1)} custom-call(bf16[4,9,192,128]{3,2,1,0:T(8,128)(2,1)} %get-tuple-element.33.i_ref.refs_0_.refs_1_.refs_2_.refs_5_.refs_6_.refs_7_, bf16[4,9,192,128]{3,2,1,0:T(8,128)(2,1)} %get-tuple-element.33.i_ref.refs_0_.refs_1_.refs_2_.refs_5_.refs_6_.refs_7_, ...), custom_call_target="tpu_custom_call" | custom-call | tf_op jit(solution)/shard_map/pallas_call | solution.py:130
  140.3 0.0 copy-done
  140.3 19.3 %conditional.11 = (bf16[4,2,192,128]{3,2,1,0:T(8,128)(2,1)}) conditional(s32[]{:T(128)} %convert_element_type.2, () %tuple.41, bf16[4,2,192,128]{3,2,1,0:T(8,128)(2,1)S(1)} %shard_map.43), branch_computations={%region_10.0_spmd, %region_11.0_spmd} | conditional | bytes 786440 | solution.py:201
  140.3 19.3 %all_to_all.29 = bf16[4,2,192,128]{3,2,1,0:T(8,128)(2,1)} all-to-all(bf16[4,2,192,128]{3,2,1,0:T(8,128)(2,1)S(1)} %param.11), channel_id=1, replica_groups=mesh['dp'=8,'tm'=8,'y'=4,'zh'=2] {'y'}, dimensions={0} | all-to-all | bytes 786432 | tf_op jit(solution)/shard_map/cond/branch_1_fun/all_to_all | solution.py:203
  159.6 3.4 %collective-permute-done.2.refs_2_ = bf16[4,192,128]{2,1,0:T(8,128)(2,1)} collective-permute-done((bf16[4,192,128]{2,1,0:T(8,128)(2,1)S(1)}, bf16[4,192,128]{2,1,0:T(8,128)(2,1)}, u32[]{:S(2)}, u32[]{:S(2)}) %collective-permute-start.2) | collective-permute-done | bytes 196640 | tf_op jit(solution)/shard_map/ppermute | solution.py:210
  163.0 2.2 %shard_map.44 = bf16[1,192,3072]{2,1,0:T(8,128)(2,1)} custom-call(bf16[4,2,192,128]{3,2,1,0:T(8,128)(2,1)} %get-tuple-element.38.refs_0_, bf16[4,2,192,128]{3,2,1,0:T(8,128)(2,1)} %copy-done, bf16[4,192,128]{2,1,0:T(8,128)(2,1)} %collective-permute-done.2.refs_2_, bf16[1,192,3072]{2,1,0:T(8,128)(2,1)} %shard_map.41.refs_6_.refs_3_), custom_call_target="tpu_custom_call", output_to_operand_aliasing={{}: (3, {})} | custom-call | tf_op jit(solution)/shard_map/pallas_call | solution.py:70
  (1 shorter events, 0.0 us)
Async XLA Ops:
  2.0 95.2 %collective-permute-start.1 = (bf16[4,3,192,128]{3,2,1,0:T(8,128)(2,1)}, bf16[4,3,192,128]{3,2,1,0:T(8,128)(2,1)}, u32[]{:S(2)}, u32[]{:S(2)}) collective-permute-start(bf16[4,3,192,128]{3,2,1,0:T(8,128)(2,1)} %shard_map.37.refs_15_), channel_id=1, source_target_pairs={{0,1},{1,0},{2,3},{3,2},{4,5},{5,4},{6,7},{7,6},{8,9},{9,8},{10,11... | collective-permute-start | bytes 1769480 | tf_op jit(solution)/shard_map/ppermute | solution.py:210
  51.5 84.3 %collective-permute-start = (bf16[4,4,192,128]{3,2,1,0:T(8,128)(2,1)}, bf16[4,4,192,128]{3,2,1,0:T(8,128)(2,1)}, u32[]{:S(2)}, u32[]{:S(2)}) collective-permute-start(bf16[4,4,192,128]{3,2,1,0:T(8,128)(2,1)} %shard_map.39), channel_id=1, source_target_pairs={{0,1},{1,0},{2,3},{3,2},{4,5},{5,4},{6,7},{7,6},{8,9},{9,8},{10,11... | collective-permute-start | bytes 2359304 | tf_op jit(solution)/shard_map/ppermute | solution.py:210
  123.1 17.2 %copy-start = (bf16[4,2,192,128]{3,2,1,0:T(8,128)(2,1)}, bf16[4,2,192,128]{3,2,1,0:T(8,128)(2,1)S(1)}, u32[]{:S(2)}) copy-start(bf16[4,2,192,128]{3,2,1,0:T(8,128)(2,1)S(1)} %get-tuple-element.37.refs_10_.refs_1_) | copy-start | bytes 1179652
  123.1 39.9 %collective-permute-start.2 = (bf16[4,192,128]{2,1,0:T(8,128)(2,1)S(1)}, bf16[4,192,128]{2,1,0:T(8,128)(2,1)}, u32[]{:S(2)}, u32[]{:S(2)}) collective-permute-start(bf16[4,192,128]{2,1,0:T(8,128)(2,1)S(1)} %slice_bitcast_fusion), channel_id=1, source_target_pairs={{0,1},{1,0},{2,3},{3,2},{4,5},{5,4},{6,7},{7,6},{8,9},{9,8},{10,11... | collective-permute-start | bytes 589832 | tf_op jit(solution)/shard_map/ppermute | solution.py:210

commit v4 on v3

--- a/solution.py
+++ b/solution.py
@@ -15,8 +15,7 @@
 SCALE = 1.0 / math.sqrt(DH)
 SCALE2 = SCALE * math.log2(math.e)
 ANY = pl.BlockSpec(memory_space=pl.ANY)
-PARAMS = pltpu.CompilerParams(vmem_limit_bytes=66_900_000)
-SMALL = pltpu.CompilerParams(vmem_limit_bytes=60 * 1024 * 1024)
+PARAMS = pltpu.CompilerParams(vmem_limit_bytes=60 * 1024 * 1024)
 COST = pl.CostEstimate(flops=0, bytes_accessed=0, transcendentals=0)
 
 
@@ -48,35 +47,38 @@
     )(half, *[array for array, _ in sources], *after)
 
 
-def here(ref):
-    if isinstance(ref, tuple):
-        return jnp.where(lax.axis_index("zh") == 0, ref[0], ref[1])
-    return ref
-
-
-def unpack(pieces, plan, first, rows, width, base=None):
+def unpack(half, pieces, plan, rows, width, base=None):
     count = len(pieces)
     extra = [] if base is None else [base]
 
-    def body(*refs):
+    def column(i, half_ref):
+        place = jnp.int32(0)
+        for n, ((a, b), _) in enumerate(plan):
+            place = jnp.where(i == n, a + b * half_ref[0], place)
+        return (0, 0, place)
+
+    def body(half_ref, *refs):
         out = refs[count + len(extra)]
-        for n, place in enumerate(plan):
-            if isinstance(place[0], tuple):
-                head = here(tuple(refs[p][index] for p, index in place))
-            else:
-                head = refs[place[0]][place[1]]
-            out[0, :, pl.ds(n * DH, DH)] = head
+        for n, (_, heads) in enumerate(plan):
+
+            @pl.when(pl.program_id(0) == n)
+            def _write(heads=heads):
+                for y, (p, index) in enumerate(heads):
+                    out[0, :, pl.ds(y * DH, DH)] = refs[p][index]
 
     return pl.pallas_call(
         body,
-        grid=(1,),
+        grid_spec=pltpu.PrefetchScalarGridSpec(
+            num_scalar_prefetch=1,
+            grid=(len(plan),),
+            in_specs=[whole(p.shape) for p in pieces] + [ANY] * len(extra),
+            out_specs=pl.BlockSpec((1, rows, Y * DH), column),
+        ),
         out_shape=jax.ShapeDtypeStruct((1, rows, width), jnp.bfloat16),
-        in_specs=[whole(p.shape) for p in pieces] + [ANY] * len(extra),
-        out_specs=pl.BlockSpec((1, rows, len(plan) * DH), lambda i: (0, 0, first // len(plan))),
-        input_output_aliases={count: 0} if extra else {},
-        compiler_params=PARAMS,
-        cost_estimate=COST,
-    )(*pieces, *extra)
+        input_output_aliases={1 + count: 0} if extra else {},
+        compiler_params=PARAMS,
+        cost_estimate=COST,
+    )(half, *pieces, *extra)
 
 
 def scores_of(q, k):
@@ -113,7 +115,7 @@
         o_ref[:, n] = jnp.concatenate(outs[n * parts : (n + 1) * parts]).reshape(Y, rows, DH)
 
 
-def attend(jobs, slots, slot=0, base=None, after=(), limit=PARAMS):
+def attend(jobs, slots, slot=0, base=None, after=()):
     operands, indices = [], []
 
     def use(array, n):
@@ -139,7 +141,7 @@
             (Y, len(jobs), rows, DH), lambda i: (0, slot // len(jobs), 0, 0)
         ),
         input_output_aliases={len(operands): 0} if extra else {},
-        compiler_params=limit,
+        compiler_params=PARAMS,
         cost_estimate=COST,
     )(*[array for array, _ in operands], *extra, *after)
 
@@ -201,7 +203,7 @@
     return lax.cond(
         lax.axis_index("dp") < 8,
         lambda a: lax.all_to_all(a, axis, split_axis=0, concat_axis=0, tiled=True),
-        jnp.zeros_like,
+        lambda a: a,
         array,
     )
 
@@ -237,25 +239,32 @@
         (raw,),
     )
     mixed = over("y", more)
-    far01 = across(take(mixed, 0, 4))
-    frames_out = over("tm", attend_frames(over("tm", trio)))
-    early = unpack([frames_out], [(0, h) for h in range(HT)], HS, rows, width)
+    far0 = across(take(mixed, 0, 2))
+    trio = over("tm", trio)
+    far1 = across(take(mixed, 2, 2, (trio,)))
+    frames_out = over("tm", attend_frames(trio))
+    early = unpack(
+        half,
+        [frames_out],
+        [((HS // Y + g, 0), [(0, g * Y + y) for y in range(Y)]) for g in range(HT // Y)],
+        rows,
+        width,
+    )
     far = over("y", far_raw)
     own = over(
         "y",
         attend(
-            [((mixed, 6), (mixed, 7), (far, 1)), ((far, 0), (mixed, 7), (far, 1))], 2, after=(early,), limit=SMALL
+            [((mixed, 6), (mixed, 7), (far, 1)), ((far, 0), (mixed, 7), (far, 1))], 2, after=(early,)
         ),
     )
     back = across(own[:, 1])
-    jobs = [((mixed, 4 + j), (mixed, 2 * j), (far01, 2 * j)) for j in range(2)]
-    pairs = over("y", attend(jobs, 2, after=(own,), limit=SMALL))
+    pairs = attend([((mixed, 4), (mixed, 0), (far0, 0))], 2, after=(own,))
+    pairs = over("y", attend([((mixed, 5), (mixed, 2), (far1, 0))], 2, 1, pairs))
     return unpack(
+        half,
         [pairs, own, back],
-        [(0, (y, j)) for j in range(2) for y in range(Y)]
-        + [((1, (y, 0)), (2, y)) for y in range(Y)]
-        + [((2, y), (1, (y, 0))) for y in range(Y)],
-        0,
+        [((j, 0), [(0, (y, j)) for y in range(Y)]) for j in range(2)]
+        + [((2, 1), [(1, (y, 0)) for y in range(Y)]), ((3, -1), [(2, y) for y in range(Y)])],
         rows,
         width,
         early,

time: 166 us -> 164 us (0.988)
  the two profiles are of different devices: /device:TPU:1 before, /device:TPU:64 now
where the time goes in v4:
time: 164 us
  blocking collectives  98.1 us (60%)
  starting transfers between devices  30.6 us (19%)
  Pallas kernels  23.2 us (14%)
  waiting for transfers between devices  9.71 us (6%)
  local copies, waits for them, and re-layouts  1.98 us (1%)
    all_to_all x6, blocking collectives, over(): lax.all_to_all(a, axis, split_axis=0, concat_axis=0, tiled=True)  98.1 us
    ppermute x4, starting transfers between devices, across(): return lax.ppermute(array, 'zh', [(0, 1), (1, 0)])  30.6 us
    ppermute x4, waiting for transfers between devices, across(): return lax.ppermute(array, 'zh', [(0, 1), (1, 0)])  9.71 us
    pallas_call x3, Pallas kernels, attend(): pl.pallas_call(functools.partial(attend_body, indices), grid=(1,), out_sh...  8.23 us
    pallas_call x2, Pallas kernels, pack(): pl.pallas_call(body, grid_spec=pltpu.PrefetchScalarGridSpec(num_scalar_pr...  4.45 us
    pallas_call x2, Pallas kernels, unpack(): pl.pallas_call(body, grid_spec=pltpu.PrefetchScalarGridSpec(num_scalar_pr...  4.22 us
    pallas_call x1, Pallas kernels, attend_frames(): pl.pallas_call(frames_body, grid=(rows // tokens,), out_shape=jax.ShapeDt...  3.7 us
  transfers between devices with their start and end apart: 4, of which 1 were waited for; matrix products, arithmetic and copies ran while one was open for 1% of the time, Pallas kernels for 11%

profile of v4, /device:TPU:64, one launch (start us, length us, event | category | flops | bytes accessed | tf_op | source)
XLA Modules:
  0.0 163.8 jit_solution(16514888920654608093)
XLA Ops:
  0.0 2.0 %shard_map.37.refs_15_ = bf16[4,3,192,128]{3,2,1,0:T(8,128)(2,1)} custom-call(s32[1]{0:T(128)} %bitcast.half_ref, bf16[1,192,3072]{2,1,0:T(8,128)(2,1)} %refs_12_.1, bf16[1,192,3072]{2,1,0:T(8,128)(2,1)} %refs_13_.1, bf16[1,192,3072]{2,1,0:T(8,128)(2,1)} %refs_14_.1), custom_call_target="tpu_custom_call" | custom-call | tf_op jit(solution)/shard_map/pallas_call | solution.py:36
  2.0 13.9 %collective-permute-start.2 = (bf16[4,3,192,128]{3,2,1,0:T(8,128)(2,1)}, bf16[4,3,192,128]{3,2,1,0:T(8,128)(2,1)S(1)}, u32[]{:S(2)}, u32[]{:S(2)}) collective-permute-start(bf16[4,3,192,128]{3,2,1,0:T(8,128)(2,1)} %shard_map.37.refs_15_), channel_id=1, source_target_pairs={{0,1},{1,0},{2,3},{3,2},{4,5},{5,4},{6,7},{7,6},{8,9},{9,8},{10,11... | collective-permute-start | bytes 1769480 | tf_op jit(solution)/shard_map/ppermute | solution.py:212
  15.9 2.4 %shard_map.38 = (bf16[4,9,192,128]{3,2,1,0:T(8,128)(2,1)S(1)}, bf16[8,3,192,128]{3,2,1,0:T(8,128)(2,1)S(1)}) custom-call(s32[1]{0:T(128)} %bitcast.half_ref, bf16[1,192,3072]{2,1,0:T(8,128)(2,1)} %refs_13_.1, bf16[1,192,3072]{2,1,0:T(8,128)(2,1)} %refs_14_.1, bf16[1,192,3072]{2,1,0:T(8,128)(2,1)} %refs_13_.1, bf16[1,192,3072]{2,1,0:T(8,128)(2,1)} %refs_14_.1, ...), custom_call_target="tpu_custom_call" | custom-call | tf_op jit(solution)/shard_map/pallas_call | solution.py:36
  18.4 26.9 %conditional.6 = (bf16[4,9,192,128]{3,2,1,0:T(8,128)(2,1)S(1)}) conditional(s32[]{:T(128)} %convert_element_type.2, bf16[4,9,192,128]{3,2,1,0:T(8,128)(2,1)S(1)} %get-tuple-element.37, bf16[4,9,192,128]{3,2,1,0:T(8,128)(2,1)S(1)} %get-tuple-element.37), branch_computations={%region_0.0_spmd, %region_1.0_spmd} | conditional | bytes 7077896 | solution.py:203
  18.4 0.1 copy.22
  18.5 26.8 %all_to_all.24 = bf16[4,9,192,128]{3,2,1,0:T(8,128)(2,1)S(1)} all-to-all(bf16[4,9,192,128]{3,2,1,0:T(8,128)(2,1)S(1)} %copy.22), channel_id=1, replica_groups=mesh['dp'=8,'tm'=8,'y'=4,'zh'=2] {'y'}, dimensions={0} | all-to-all | bytes 3538944 | tf_op jit(solution)/shard_map/cond/branch_1_fun/all_to_all | solution.py:205
  45.3 1.3 shard_map.40
  46.6 2.2 %collective-permute-start.1 = (bf16[4,2,192,128]{3,2,1,0:T(8,128)(2,1)}, bf16[4,2,192,128]{3,2,1,0:T(8,128)(2,1)}, u32[]{:S(2)}, u32[]{:S(2)}) collective-permute-start(bf16[4,2,192,128]{3,2,1,0:T(8,128)(2,1)} %shard_map.40), channel_id=1, source_target_pairs={{0,1},{1,0},{2,3},{3,2},{4,5},{5,4},{6,7},{7,6},{8,9},{9,8},{10,11... | collective-permute-start | bytes 1179656 | tf_op jit(solution)/shard_map/ppermute | solution.py:212
  48.8 21.7 %conditional.7 = (bf16[8,3,192,128]{3,2,1,0:T(8,128)(2,1)S(1)}) conditional(s32[]{:T(128)} %convert_element_type.2, bf16[8,3,192,128]{3,2,1,0:T(8,128)(2,1)S(1)} %get-tuple-element.38, bf16[8,3,192,128]{3,2,1,0:T(8,128)(2,1)S(1)} %get-tuple-element.38), branch_computations={%region_2.0_spmd, %region_3.0_spmd} | conditional | bytes 4718600 | solution.py:203
  48.8 0.1 copy.23
  48.9 21.6 %all_to_all.25 = bf16[8,3,192,128]{3,2,1,0:T(8,128)(2,1)S(1)} all-to-all(bf16[8,3,192,128]{3,2,1,0:T(8,128)(2,1)S(1)} %copy.23), channel_id=1, replica_groups=mesh['dp'=8,'tm'=8,'y'=4,'zh'=2] {'tm'}, dimensions={0} | all-to-all | bytes 2359296 | tf_op jit(solution)/shard_map/cond/branch_1_fun/all_to_all | solution.py:205
  70.5 1.3 shard_map.39
  71.8 12.3 %collective-permute-start = (bf16[4,2,192,128]{3,2,1,0:T(8,128)(2,1)}, bf16[4,2,192,128]{3,2,1,0:T(8,128)(2,1)}, u32[]{:S(2)}, u32[]{:S(2)}) collective-permute-start(bf16[4,2,192,128]{3,2,1,0:T(8,128)(2,1)} %shard_map.39), channel_id=1, source_target_pairs={{0,1},{1,0},{2,3},{3,2},{4,5},{5,4},{6,7},{7,6},{8,9},{9,8},{10,11... | collective-permute-start | bytes 1179656 | tf_op jit(solution)/shard_map/ppermute | solution.py:212
  84.2 3.7 %shard_map.41 = bf16[8,192,128]{2,1,0:T(8,128)(2,1)} custom-call(bf16[8,3,192,128]{3,2,1,0:T(8,128)(2,1)S(1)} %get-tuple-element.40.refs_0_.q_ref.k_ref.v_ref, bf16[8,3,192,128]{3,2,1,0:T(8,128)(2,1)S(1)} %get-tuple-element.40.refs_0_.q_ref.k_ref.v_ref, bf16[8,3,192,128]{3,2,1,0:T(8,128)(2,1)S(1)} %get-tuple-element.40.refs_0_.q_ref.k_ref.v_ref), custom_call_target="tpu_custom_call" | custom-call | tf_op jit(solution)/shard_map/pallas_call | solution.py:191
  87.9 13.0 %conditional.9 = (bf16[8,192,128]{2,1,0:T(8,128)(2,1)}) conditional(s32[]{:T(128)} %convert_element_type.2, bf16[8,192,128]{2,1,0:T(8,128)(2,1)} %shard_map.41, bf16[8,192,128]{2,1,0:T(8,128)(2,1)} %shard_map.41), branch_computations={%region_6.0_spmd, %region_7.0_spmd} | conditional | bytes 1572872 | solution.py:203
  87.9 1.0 copy.25
  88.9 12.0 %all_to_all.27 = bf16[8,192,128]{2,1,0:T(8,128)(2,1)} all-to-all(bf16[8,192,128]{2,1,0:T(8,128)(2,1)S(1)} %copy.25), channel_id=1, replica_groups=mesh['dp'=8,'tm'=8,'y'=4,'zh'=2] {'tm'}, dimensions={0} | all-to-all | bytes 786432 | tf_op jit(solution)/shard_map/cond/branch_1_fun/all_to_all | solution.py:205
  100.9 1.8 %shard_map.42.refs_6_.refs_3_ = bf16[1,192,3072]{2,1,0:T(8,128)(2,1)} custom-call(s32[1]{0:T(128)} %bitcast.half_ref, bf16[8,192,128]{2,1,0:T(8,128)(2,1)} %get-tuple-element.42.refs_0_), custom_call_target="tpu_custom_call" | custom-call | tf_op jit(solution)/shard_map/pallas_call | solution.py:69
  102.7 0.0 collective-permute-done.2
  102.7 13.0 %conditional.8 = (bf16[4,3,192,128]{3,2,1,0:T(8,128)(2,1)S(1)}) conditional(s32[]{:T(128)} %convert_element_type.2, bf16[4,3,192,128]{3,2,1,0:T(8,128)(2,1)S(1)} %collective-permute-done.2, bf16[4,3,192,128]{3,2,1,0:T(8,128)(2,1)S(1)} %collective-permute-done.2), branch_computations={%region_4.0_spmd, %region_5.0_spmd} | conditional | bytes 2359304 | solution.py:203
  102.7 12.9 %all_to_all.26 = bf16[4,3,192,128]{3,2,1,0:T(8,128)(2,1)S(1)} all-to-all(bf16[4,3,192,128]{3,2,1,0:T(8,128)(2,1)S(1)} %copy.24), channel_id=1, replica_groups=mesh['dp'=8,'tm'=8,'y'=4,'zh'=2] {'y'}, dimensions={0} | all-to-all | bytes 1179648 | tf_op jit(solution)/shard_map/cond/branch_1_fun/all_to_all | solution.py:205
  115.7 3.0 %shard_map.43 = bf16[4,2,192,128]{3,2,1,0:T(8,128)(2,1)S(1)} custom-call(bf16[4,9,192,128]{3,2,1,0:T(8,128)(2,1)S(1)} %get-tuple-element.39.i_ref.refs_0_.refs_1_.refs_2_, bf16[4,9,192,128]{3,2,1,0:T(8,128)(2,1)S(1)} %get-tuple-element.39.i_ref.refs_0_.refs_1_.refs_2_, bf16[4,9,192,128]{3,2,1,0:T(8,128)(2,1)S(1)} %get-tuple-element.39.i_ref.refs_0_.refs_1_.refs_2_, ...), custom_call_target="tpu_custom_call" | custom-call | tf_op jit(solution)/shard_map/pallas_call | solution.py:132
  118.7 10.1 %conditional.10 = (bf16[4,2,192,128]{3,2,1,0:T(8,128)(2,1)S(1)}) conditional(s32[]{:T(128)} %convert_element_type.2, bf16[4,2,192,128]{3,2,1,0:T(8,128)(2,1)S(1)} %shard_map.43, bf16[4,2,192,128]{3,2,1,0:T(8,128)(2,1)S(1)} %shard_map.43), branch_computations={%region_8.0_spmd, %region_9.0_spmd} | conditional | bytes 1572872 | solution.py:203
  118.7 10.1 %all_to_all.28 = bf16[4,2,192,128]{3,2,1,0:T(8,128)(2,1)S(1)} all-to-all(bf16[4,2,192,128]{3,2,1,0:T(8,128)(2,1)S(1)} %copy.26), channel_id=1, replica_groups=mesh['dp'=8,'tm'=8,'y'=4,'zh'=2] {'y'}, dimensions={0} | all-to-all | bytes 786432 | tf_op jit(solution)/shard_map/cond/branch_1_fun/all_to_all | solution.py:205
  128.8 2.2 %collective-permute-start.3 = (bf16[4,192,128]{2,1,0:T(8,128)(2,1)S(1)}, bf16[4,192,128]{2,1,0:T(8,128)(2,1)S(1)}, u32[]{:S(2)}, u32[]{:S(2)}) collective-permute-start(bf16[4,192,128]{2,1,0:T(8,128)(2,1)S(1)} %slice_bitcast_fusion), channel_id=1, source_target_pairs={{0,1},{1,0},{2,3},{3,2},{4,5},{5,4},{6,7},{7,6},{8,9},{9,8},{10,11... | collective-permute-start | bytes 589832 | tf_op jit(solution)/shard_map/ppermute | solution.py:212
  131.0 2.6 %shard_map.44.refs_5_ = bf16[4,2,192,128]{3,2,1,0:T(8,128)(2,1)S(1)} custom-call(bf16[4,9,192,128]{3,2,1,0:T(8,128)(2,1)S(1)} %get-tuple-element.39.i_ref.refs_0_.refs_1_.refs_2_, bf16[4,9,192,128]{3,2,1,0:T(8,128)(2,1)S(1)} %get-tuple-element.39.i_ref.refs_0_.refs_1_.refs_2_, bf16[4,9,192,128]{3,2,1,0:T(8,128)(2,1)S(1)} %get-tuple-element.39.i_ref.refs_0_.refs_1_.refs_2_, ...), custom_call_target="tpu_custom_call" | custom-call | tf_op jit(solution)/shard_map/pallas_call | solution.py:132
  133.7 9.7 %collective-permute-done.refs_3_.refs_4_ = bf16[4,2,192,128]{3,2,1,0:T(8,128)(2,1)} collective-permute-done((bf16[4,2,192,128]{3,2,1,0:T(8,128)(2,1)}, bf16[4,2,192,128]{3,2,1,0:T(8,128)(2,1)}, u32[]{:S(2)}, u32[]{:S(2)}) %collective-permute-start) | collective-permute-done | bytes 393248 | tf_op jit(solution)/shard_map/ppermute | solution.py:212
  143.4 2.6 %shard_map.45 = bf16[4,2,192,128]{3,2,1,0:T(8,128)(2,1)S(1)} custom-call(bf16[4,9,192,128]{3,2,1,0:T(8,128)(2,1)S(1)} %get-tuple-element.39.i_ref.refs_0_.refs_1_.refs_2_, bf16[4,9,192,128]{3,2,1,0:T(8,128)(2,1)S(1)} %get-tuple-element.39.i_ref.refs_0_.refs_1_.refs_2_, ...), custom_call_target="tpu_custom_call", output_to_operand_aliasing={{}: (5, {})} | custom-call | tf_op jit(solution)/shard_map/pallas_call | solution.py:132
  146.0 14.7 %conditional.11 = (bf16[4,2,192,128]{3,2,1,0:T(8,128)(2,1)S(1)}) conditional(s32[]{:T(128)} %convert_element_type.2, bf16[4,2,192,128]{3,2,1,0:T(8,128)(2,1)S(1)} %shard_map.45, bf16[4,2,192,128]{3,2,1,0:T(8,128)(2,1)S(1)} %shard_map.45), branch_computations={%region_10.0_spmd, %region_11.0_spmd} | conditional | bytes 1572872 | solution.py:203
  146.0 14.6 %all_to_all.29 = bf16[4,2,192,128]{3,2,1,0:T(8,128)(2,1)S(1)} all-to-all(bf16[4,2,192,128]{3,2,1,0:T(8,128)(2,1)S(1)} %copy.27), channel_id=1, replica_groups=mesh['dp'=8,'tm'=8,'y'=4,'zh'=2] {'y'}, dimensions={0} | all-to-all | bytes 786432 | tf_op jit(solution)/shard_map/cond/branch_1_fun/all_to_all | solution.py:205
  160.7 0.7 copy-done
  161.4 2.4 %shard_map.46 = bf16[1,192,3072]{2,1,0:T(8,128)(2,1)} custom-call(s32[1]{0:T(128)} %bitcast.half_ref, bf16[4,2,192,128]{3,2,1,0:T(8,128)(2,1)S(1)} %get-tuple-element.44.refs_0_, bf16[4,2,192,128]{3,2,1,0:T(8,128)(2,1)S(1)} %get-tuple-element.43.refs_5_.refs_1_, bf16[4,192,128]{2,1,0:T(8,128)(2,1)} %copy-done, ...), custom_call_target="tpu_custom_call", output_to_operand_aliasing={{}: (4, {})} | custom-call | tf_op jit(solution)/shard_map/pallas_call | solution.py:69
  (7 shorter events, 0.1 us)
Async XLA Ops:
  2.0 100.6 %collective-permute-start.2 = (bf16[4,3,192,128]{3,2,1,0:T(8,128)(2,1)}, bf16[4,3,192,128]{3,2,1,0:T(8,128)(2,1)S(1)}, u32[]{:S(2)}, u32[]{:S(2)}) collective-permute-start(bf16[4,3,192,128]{3,2,1,0:T(8,128)(2,1)} %shard_map.37.refs_15_), channel_id=1, source_target_pairs={{0,1},{1,0},{2,3},{3,2},{4,5},{5,4},{6,7},{7,6},{8,9},{9,8},{10,11... | collective-permute-start | bytes 1769480 | tf_op jit(solution)/shard_map/ppermute | solution.py:212
  46.6 84.4 %collective-permute-start.1 = (bf16[4,2,192,128]{3,2,1,0:T(8,128)(2,1)}, bf16[4,2,192,128]{3,2,1,0:T(8,128)(2,1)}, u32[]{:S(2)}, u32[]{:S(2)}) collective-permute-start(bf16[4,2,192,128]{3,2,1,0:T(8,128)(2,1)} %shard_map.40), channel_id=1, source_target_pairs={{0,1},{1,0},{2,3},{3,2},{4,5},{5,4},{6,7},{7,6},{8,9},{9,8},{10,11... | collective-permute-start | bytes 1179656 | tf_op jit(solution)/shard_map/ppermute | solution.py:212
  71.8 71.5 %collective-permute-start = (bf16[4,2,192,128]{3,2,1,0:T(8,128)(2,1)}, bf16[4,2,192,128]{3,2,1,0:T(8,128)(2,1)}, u32[]{:S(2)}, u32[]{:S(2)}) collective-permute-start(bf16[4,2,192,128]{3,2,1,0:T(8,128)(2,1)} %shard_map.39), channel_id=1, source_target_pairs={{0,1},{1,0},{2,3},{3,2},{4,5},{5,4},{6,7},{7,6},{8,9},{9,8},{10,11... | collective-permute-start | bytes 1179656 | tf_op jit(solution)/shard_map/ppermute | solution.py:212
  128.8 31.8 %collective-permute-start.3 = (bf16[4,192,128]{2,1,0:T(8,128)(2,1)S(1)}, bf16[4,192,128]{2,1,0:T(8,128)(2,1)S(1)}, u32[]{:S(2)}, u32[]{:S(2)}) collective-permute-start(bf16[4,192,128]{2,1,0:T(8,128)(2,1)S(1)} %slice_bitcast_fusion), channel_id=1, source_target_pairs={{0,1},{1,0},{2,3},{3,2},{4,5},{5,4},{6,7},{7,6},{8,9},{9,8},{10,11... | collective-permute-start | bytes 589832 | tf_op jit(solution)/shard_map/ppermute | solution.py:212
  160.7 0.7 copy-start

commit v5 on v3

--- a/solution.py
+++ b/solution.py
@@ -15,8 +15,8 @@
 SCALE = 1.0 / math.sqrt(DH)
 SCALE2 = SCALE * math.log2(math.e)
 ANY = pl.BlockSpec(memory_space=pl.ANY)
-PARAMS = pltpu.CompilerParams(vmem_limit_bytes=66_900_000)
-SMALL = pltpu.CompilerParams(vmem_limit_bytes=60 * 1024 * 1024)
+PARAMS = pltpu.CompilerParams(vmem_limit_bytes=60 * 1024 * 1024)
+LAST = pltpu.CompilerParams(vmem_limit_bytes=66_900_000)
 COST = pl.CostEstimate(flops=0, bytes_accessed=0, transcendentals=0)
 
 
@@ -54,7 +54,7 @@
     return ref
 
 
-def unpack(pieces, plan, first, rows, width, base=None):
+def unpack(pieces, plan, first, rows, width, base=None, limit=PARAMS):
     count = len(pieces)
     extra = [] if base is None else [base]
 
@@ -74,7 +74,7 @@
         in_specs=[whole(p.shape) for p in pieces] + [ANY] * len(extra),
         out_specs=pl.BlockSpec((1, rows, len(plan) * DH), lambda i: (0, 0, first // len(plan))),
         input_output_aliases={count: 0} if extra else {},
-        compiler_params=PARAMS,
+        compiler_params=limit,
         cost_estimate=COST,
     )(*pieces, *extra)
 
@@ -113,7 +113,7 @@
         o_ref[:, n] = jnp.concatenate(outs[n * parts : (n + 1) * parts]).reshape(Y, rows, DH)
 
 
-def attend(jobs, slots, slot=0, base=None, after=(), limit=PARAMS):
+def attend(jobs, slots, slot=0, base=None, after=()):
     operands, indices = [], []
 
     def use(array, n):
@@ -139,7 +139,7 @@
             (Y, len(jobs), rows, DH), lambda i: (0, slot // len(jobs), 0, 0)
         ),
         input_output_aliases={len(operands): 0} if extra else {},
-        compiler_params=limit,
+        compiler_params=PARAMS,
         cost_estimate=COST,
     )(*[array for array, _ in operands], *extra, *after)
 
@@ -201,7 +201,7 @@
     return lax.cond(
         lax.axis_index("dp") < 8,
         lambda a: lax.all_to_all(a, axis, split_axis=0, concat_axis=0, tiled=True),
-        jnp.zeros_like,
+        lambda a: a,
         array,
     )
 
@@ -237,19 +237,21 @@
         (raw,),
     )
     mixed = over("y", more)
-    far01 = across(take(mixed, 0, 4))
-    frames_out = over("tm", attend_frames(over("tm", trio)))
+    far0 = across(take(mixed, 0, 2))
+    trio = over("tm", trio)
+    far1 = across(take(mixed, 2, 2, (trio,)))
+    frames_out = over("tm", attend_frames(trio))
     early = unpack([frames_out], [(0, h) for h in range(HT)], HS, rows, width)
     far = over("y", far_raw)
     own = over(
         "y",
         attend(
-            [((mixed, 6), (mixed, 7), (far, 1)), ((far, 0), (mixed, 7), (far, 1))], 2, after=(early,), limit=SMALL
+            [((mixed, 6), (mixed, 7), (far, 1)), ((far, 0), (mixed, 7), (far, 1))], 2, after=(early,)
         ),
     )
     back = across(own[:, 1])
-    jobs = [((mixed, 4 + j), (mixed, 2 * j), (far01, 2 * j)) for j in range(2)]
-    pairs = over("y", attend(jobs, 2, after=(own,), limit=SMALL))
+    pairs = attend([((mixed, 4), (mixed, 0), (far0, 0))], 2, after=(own,))
+    pairs = over("y", attend([((mixed, 5), (mixed, 2), (far1, 0))], 2, 1, pairs))
     return unpack(
         [pairs, own, back],
         [(0, (y, j)) for j in range(2) for y in range(Y)]
@@ -259,6 +261,7 @@
         rows,
         width,
         early,
+        LAST,
     )
 
 

time: 166 us -> 165 us (level)
  the two profiles are of different devices: /device:TPU:1 before, /device:TPU:64 now
where the time goes in v5:
time: 165 us
  blocking collectives  98.5 us (60%)
  starting transfers between devices  30.6 us (19%)
  Pallas kernels  24.4 us (15%)
  waiting for transfers between devices  8.58 us (5%)
  local copies, waits for them, and re-layouts  2.27 us (1%)
    all_to_all x6, blocking collectives, over(): lax.all_to_all(a, axis, split_axis=0, concat_axis=0, tiled=True)  98.5 us
    ppermute x4, starting transfers between devices, across(): return lax.ppermute(array, 'zh', [(0, 1), (1, 0)])  30.6 us
    pallas_call x3, Pallas kernels, attend(): pl.pallas_call(functools.partial(attend_body, indices), grid=(1,), out_sh...  9.52 us
    ppermute x4, waiting for transfers between devices, across(): return lax.ppermute(array, 'zh', [(0, 1), (1, 0)])  8.58 us
    pallas_call x2, Pallas kernels, pack(): pl.pallas_call(body, grid_spec=pltpu.PrefetchScalarGridSpec(num_scalar_pr...  4.45 us
    pallas_call x2, Pallas kernels, unpack(): pl.pallas_call(body, grid=(1,), out_shape=jax.ShapeDtypeStruct((1, rows,...  4.08 us
    pallas_call x1, Pallas kernels, attend_frames(): pl.pallas_call(frames_body, grid=(rows // tokens,), out_shape=jax.ShapeDt...  3.7 us
  transfers between devices with their start and end apart: 4, of which 1 were waited for; matrix products, arithmetic and copies ran while one was open for 1% of the time, Pallas kernels for 12%

profile of v5, /device:TPU:64, one launch (start us, length us, event | category | flops | bytes accessed | tf_op | source)
XLA Modules:
  0.0 164.6 jit_solution(18051675984377783485)
XLA Ops:
  0.0 2.0 %shard_map.37.refs_15_ = bf16[4,3,192,128]{3,2,1,0:T(8,128)(2,1)} custom-call(s32[1]{0:T(128)} %bitcast.half_ref, bf16[1,192,3072]{2,1,0:T(8,128)(2,1)} %refs_12_.1, bf16[1,192,3072]{2,1,0:T(8,128)(2,1)} %refs_13_.1, bf16[1,192,3072]{2,1,0:T(8,128)(2,1)} %refs_14_.1), custom_call_target="tpu_custom_call" | custom-call | tf_op jit(solution)/shard_map/pallas_call | solution.py:37
  2.0 13.9 %collective-permute-start.2 = (bf16[4,3,192,128]{3,2,1,0:T(8,128)(2,1)}, bf16[4,3,192,128]{3,2,1,0:T(8,128)(2,1)S(1)}, u32[]{:S(2)}, u32[]{:S(2)}) collective-permute-start(bf16[4,3,192,128]{3,2,1,0:T(8,128)(2,1)} %shard_map.37.refs_15_), channel_id=1, source_target_pairs={{0,1},{1,0},{2,3},{3,2},{4,5},{5,4},{6,7},{7,6},{8,9},{9,8},{10,11... | collective-permute-start | bytes 1769480 | tf_op jit(solution)/shard_map/ppermute | solution.py:210
  15.9 2.4 %shard_map.38 = (bf16[4,9,192,128]{3,2,1,0:T(8,128)(2,1)S(1)}, bf16[8,3,192,128]{3,2,1,0:T(8,128)(2,1)S(1)}) custom-call(s32[1]{0:T(128)} %bitcast.half_ref, bf16[1,192,3072]{2,1,0:T(8,128)(2,1)} %refs_13_.1, bf16[1,192,3072]{2,1,0:T(8,128)(2,1)} %refs_14_.1, bf16[1,192,3072]{2,1,0:T(8,128)(2,1)} %refs_13_.1, bf16[1,192,3072]{2,1,0:T(8,128)(2,1)} %refs_14_.1, ...), custom_call_target="tpu_custom_call" | custom-call | tf_op jit(solution)/shard_map/pallas_call | solution.py:37
  18.4 26.9 %conditional.6 = (bf16[4,9,192,128]{3,2,1,0:T(8,128)(2,1)S(1)}) conditional(s32[]{:T(128)} %convert_element_type.2, bf16[4,9,192,128]{3,2,1,0:T(8,128)(2,1)S(1)} %get-tuple-element.37, bf16[4,9,192,128]{3,2,1,0:T(8,128)(2,1)S(1)} %get-tuple-element.37), branch_computations={%region_0.0_spmd, %region_1.0_spmd} | conditional | bytes 7077896 | solution.py:201
  18.4 0.1 copy.22
  18.5 26.8 %all_to_all.24 = bf16[4,9,192,128]{3,2,1,0:T(8,128)(2,1)S(1)} all-to-all(bf16[4,9,192,128]{3,2,1,0:T(8,128)(2,1)S(1)} %copy.22), channel_id=1, replica_groups=mesh['dp'=8,'tm'=8,'y'=4,'zh'=2] {'y'}, dimensions={0} | all-to-all | bytes 3538944 | tf_op jit(solution)/shard_map/cond/branch_1_fun/all_to_all | solution.py:203
  45.3 1.3 shard_map.40
  46.6 2.2 %collective-permute-start.1 = (bf16[4,2,192,128]{3,2,1,0:T(8,128)(2,1)}, bf16[4,2,192,128]{3,2,1,0:T(8,128)(2,1)}, u32[]{:S(2)}, u32[]{:S(2)}) collective-permute-start(bf16[4,2,192,128]{3,2,1,0:T(8,128)(2,1)} %shard_map.40), channel_id=1, source_target_pairs={{0,1},{1,0},{2,3},{3,2},{4,5},{5,4},{6,7},{7,6},{8,9},{9,8},{10,11... | collective-permute-start | bytes 1179656 | tf_op jit(solution)/shard_map/ppermute | solution.py:210
  48.8 21.7 %conditional.7 = (bf16[8,3,192,128]{3,2,1,0:T(8,128)(2,1)S(1)}) conditional(s32[]{:T(128)} %convert_element_type.2, bf16[8,3,192,128]{3,2,1,0:T(8,128)(2,1)S(1)} %get-tuple-element.38, bf16[8,3,192,128]{3,2,1,0:T(8,128)(2,1)S(1)} %get-tuple-element.38), branch_computations={%region_2.0_spmd, %region_3.0_spmd} | conditional | bytes 4718600 | solution.py:201
  48.9 0.1 copy.23
  48.9 21.6 %all_to_all.25 = bf16[8,3,192,128]{3,2,1,0:T(8,128)(2,1)S(1)} all-to-all(bf16[8,3,192,128]{3,2,1,0:T(8,128)(2,1)S(1)} %copy.23), channel_id=1, replica_groups=mesh['dp'=8,'tm'=8,'y'=4,'zh'=2] {'tm'}, dimensions={0} | all-to-all | bytes 2359296 | tf_op jit(solution)/shard_map/cond/branch_1_fun/all_to_all | solution.py:203
  70.5 1.3 shard_map.39
  71.9 12.3 %collective-permute-start = (bf16[4,2,192,128]{3,2,1,0:T(8,128)(2,1)}, bf16[4,2,192,128]{3,2,1,0:T(8,128)(2,1)}, u32[]{:S(2)}, u32[]{:S(2)}) collective-permute-start(bf16[4,2,192,128]{3,2,1,0:T(8,128)(2,1)} %shard_map.39), channel_id=1, source_target_pairs={{0,1},{1,0},{2,3},{3,2},{4,5},{5,4},{6,7},{7,6},{8,9},{9,8},{10,11... | collective-permute-start | bytes 1179656 | tf_op jit(solution)/shard_map/ppermute | solution.py:210
  84.2 3.7 %shard_map.41 = bf16[8,192,128]{2,1,0:T(8,128)(2,1)} custom-call(bf16[8,3,192,128]{3,2,1,0:T(8,128)(2,1)S(1)} %get-tuple-element.40.refs_0_.q_ref.k_ref.v_ref, bf16[8,3,192,128]{3,2,1,0:T(8,128)(2,1)S(1)} %get-tuple-element.40.refs_0_.q_ref.k_ref.v_ref, bf16[8,3,192,128]{3,2,1,0:T(8,128)(2,1)S(1)} %get-tuple-element.40.refs_0_.q_ref.k_ref.v_ref), custom_call_target="tpu_custom_call" | custom-call | tf_op jit(solution)/shard_map/pallas_call | solution.py:189
  87.9 13.0 %conditional.9 = (bf16[8,192,128]{2,1,0:T(8,128)(2,1)}) conditional(s32[]{:T(128)} %convert_element_type.2, bf16[8,192,128]{2,1,0:T(8,128)(2,1)} %shard_map.41, bf16[8,192,128]{2,1,0:T(8,128)(2,1)} %shard_map.41), branch_computations={%region_6.0_spmd, %region_7.0_spmd} | conditional | bytes 1572872 | solution.py:201
  87.9 1.0 copy.25
  88.9 12.0 %all_to_all.27 = bf16[8,192,128]{2,1,0:T(8,128)(2,1)} all-to-all(bf16[8,192,128]{2,1,0:T(8,128)(2,1)S(1)} %copy.25), channel_id=1, replica_groups=mesh['dp'=8,'tm'=8,'y'=4,'zh'=2] {'tm'}, dimensions={0} | all-to-all | bytes 786432 | tf_op jit(solution)/shard_map/cond/branch_1_fun/all_to_all | solution.py:203
  100.9 1.9 %shard_map.42.refs_6_.refs_3_ = bf16[1,192,3072]{2,1,0:T(8,128)(2,1)} custom-call(bf16[8,192,128]{2,1,0:T(8,128)(2,1)} %get-tuple-element.42.refs_0_), custom_call_target="tpu_custom_call" | custom-call | tf_op jit(solution)/shard_map/pallas_call | solution.py:70
  102.8 0.0 collective-permute-done.2
  102.8 13.0 %conditional.8 = (bf16[4,3,192,128]{3,2,1,0:T(8,128)(2,1)S(1)}) conditional(s32[]{:T(128)} %convert_element_type.2, bf16[4,3,192,128]{3,2,1,0:T(8,128)(2,1)S(1)} %collective-permute-done.2, bf16[4,3,192,128]{3,2,1,0:T(8,128)(2,1)S(1)} %collective-permute-done.2), branch_computations={%region_4.0_spmd, %region_5.0_spmd} | conditional | bytes 2359304 | solution.py:201
  102.8 12.9 %all_to_all.26 = bf16[4,3,192,128]{3,2,1,0:T(8,128)(2,1)S(1)} all-to-all(bf16[4,3,192,128]{3,2,1,0:T(8,128)(2,1)S(1)} %copy.24), channel_id=1, replica_groups=mesh['dp'=8,'tm'=8,'y'=4,'zh'=2] {'y'}, dimensions={0} | all-to-all | bytes 1179648 | tf_op jit(solution)/shard_map/cond/branch_1_fun/all_to_all | solution.py:203
  115.8 3.0 %shard_map.43 = bf16[4,2,192,128]{3,2,1,0:T(8,128)(2,1)S(1)} custom-call(bf16[4,9,192,128]{3,2,1,0:T(8,128)(2,1)S(1)} %get-tuple-element.39.i_ref.refs_0_.refs_1_.refs_2_, bf16[4,9,192,128]{3,2,1,0:T(8,128)(2,1)S(1)} %get-tuple-element.39.i_ref.refs_0_.refs_1_.refs_2_, bf16[4,9,192,128]{3,2,1,0:T(8,128)(2,1)S(1)} %get-tuple-element.39.i_ref.refs_0_.refs_1_.refs_2_, ...), custom_call_target="tpu_custom_call" | custom-call | tf_op jit(solution)/shard_map/pallas_call | solution.py:130
  118.8 10.1 %conditional.10 = (bf16[4,2,192,128]{3,2,1,0:T(8,128)(2,1)S(1)}) conditional(s32[]{:T(128)} %convert_element_type.2, bf16[4,2,192,128]{3,2,1,0:T(8,128)(2,1)S(1)} %shard_map.43, bf16[4,2,192,128]{3,2,1,0:T(8,128)(2,1)S(1)} %shard_map.43), branch_computations={%region_8.0_spmd, %region_9.0_spmd} | conditional | bytes 1572872 | solution.py:201
  118.8 10.1 %all_to_all.28 = bf16[4,2,192,128]{3,2,1,0:T(8,128)(2,1)S(1)} all-to-all(bf16[4,2,192,128]{3,2,1,0:T(8,128)(2,1)S(1)} %copy.26), channel_id=1, replica_groups=mesh['dp'=8,'tm'=8,'y'=4,'zh'=2] {'y'}, dimensions={0} | all-to-all | bytes 786432 | tf_op jit(solution)/shard_map/cond/branch_1_fun/all_to_all | solution.py:203
  128.9 2.2 %collective-permute-start.3 = (bf16[4,192,128]{2,1,0:T(8,128)(2,1)S(1)}, bf16[4,192,128]{2,1,0:T(8,128)(2,1)}, u32[]{:S(2)}, u32[]{:S(2)}) collective-permute-start(bf16[4,192,128]{2,1,0:T(8,128)(2,1)S(1)} %slice_bitcast_fusion), channel_id=1, source_target_pairs={{0,1},{1,0},{2,3},{3,2},{4,5},{5,4},{6,7},{7,6},{8,9},{9,8},{10,11... | collective-permute-start | bytes 589832 | tf_op jit(solution)/shard_map/ppermute | solution.py:210
  131.2 3.3 %shard_map.44.refs_5_ = bf16[4,2,192,128]{3,2,1,0:T(8,128)(2,1)} custom-call(bf16[4,9,192,128]{3,2,1,0:T(8,128)(2,1)S(1)} %get-tuple-element.39.i_ref.refs_0_.refs_1_.refs_2_, bf16[4,9,192,128]{3,2,1,0:T(8,128)(2,1)S(1)} %get-tuple-element.39.i_ref.refs_0_.refs_1_.refs_2_, bf16[4,9,192,128]{3,2,1,0:T(8,128)(2,1)S(1)} %get-tuple-element.39.i_ref.refs_0_.refs_1_.refs_2_, ...), custom_call_target="tpu_custom_call" | custom-call | tf_op jit(solution)/shard_map/pallas_call | solution.py:130
  134.4 8.6 %collective-permute-done.refs_3_.refs_4_ = bf16[4,2,192,128]{3,2,1,0:T(8,128)(2,1)} collective-permute-done((bf16[4,2,192,128]{3,2,1,0:T(8,128)(2,1)}, bf16[4,2,192,128]{3,2,1,0:T(8,128)(2,1)}, u32[]{:S(2)}, u32[]{:S(2)}) %collective-permute-start) | collective-permute-done | bytes 393248 | tf_op jit(solution)/shard_map/ppermute | solution.py:210
  143.0 3.2 %shard_map.45 = bf16[4,2,192,128]{3,2,1,0:T(8,128)(2,1)} custom-call(bf16[4,9,192,128]{3,2,1,0:T(8,128)(2,1)S(1)} %get-tuple-element.39.i_ref.refs_0_.refs_1_.refs_2_, bf16[4,9,192,128]{3,2,1,0:T(8,128)(2,1)S(1)} %get-tuple-element.39.i_ref.refs_0_.refs_1_.refs_2_, ...), custom_call_target="tpu_custom_call", output_to_operand_aliasing={{}: (5, {})} | custom-call | tf_op jit(solution)/shard_map/pallas_call | solution.py:130
  146.3 16.1 %conditional.11 = (bf16[4,2,192,128]{3,2,1,0:T(8,128)(2,1)}) conditional(s32[]{:T(128)} %convert_element_type.2, bf16[4,2,192,128]{3,2,1,0:T(8,128)(2,1)} %shard_map.45, bf16[4,2,192,128]{3,2,1,0:T(8,128)(2,1)} %shard_map.45), branch_computations={%region_10.0_spmd, %region_11.0_spmd} | conditional | bytes 1572872 | solution.py:201
  146.3 1.0 copy.27
  147.3 15.1 %all_to_all.29 = bf16[4,2,192,128]{3,2,1,0:T(8,128)(2,1)} all-to-all(bf16[4,2,192,128]{3,2,1,0:T(8,128)(2,1)S(1)} %copy.27), channel_id=1, replica_groups=mesh['dp'=8,'tm'=8,'y'=4,'zh'=2] {'y'}, dimensions={0} | all-to-all | bytes 786432 | tf_op jit(solution)/shard_map/cond/branch_1_fun/all_to_all | solution.py:203
  162.3 2.2 %shard_map.46 = bf16[1,192,3072]{2,1,0:T(8,128)(2,1)} custom-call(bf16[4,2,192,128]{3,2,1,0:T(8,128)(2,1)} %get-tuple-element.44.refs_0_, bf16[4,2,192,128]{3,2,1,0:T(8,128)(2,1)} %copy-done, bf16[4,192,128]{2,1,0:T(8,128)(2,1)} %collective-permute-done.3.refs_2_, bf16[1,192,3072]{2,1,0:T(8,128)(2,1)} %shard_map.42.refs_6_.refs_3_), custom_call_target="tpu_custom_call", output_to_operand_aliasing={{}: (3, {})} | custom-call | tf_op jit(solution)/shard_map/pallas_call | solution.py:70
  (7 shorter events, 0.1 us)
Async XLA Ops:
  2.0 100.8 %collective-permute-start.2 = (bf16[4,3,192,128]{3,2,1,0:T(8,128)(2,1)}, bf16[4,3,192,128]{3,2,1,0:T(8,128)(2,1)S(1)}, u32[]{:S(2)}, u32[]{:S(2)}) collective-permute-start(bf16[4,3,192,128]{3,2,1,0:T(8,128)(2,1)} %shard_map.37.refs_15_), channel_id=1, source_target_pairs={{0,1},{1,0},{2,3},{3,2},{4,5},{5,4},{6,7},{7,6},{8,9},{9,8},{10,11... | collective-permute-start | bytes 1769480 | tf_op jit(solution)/shard_map/ppermute | solution.py:210
  46.6 84.5 %collective-permute-start.1 = (bf16[4,2,192,128]{3,2,1,0:T(8,128)(2,1)}, bf16[4,2,192,128]{3,2,1,0:T(8,128)(2,1)}, u32[]{:S(2)}, u32[]{:S(2)}) collective-permute-start(bf16[4,2,192,128]{3,2,1,0:T(8,128)(2,1)} %shard_map.40), channel_id=1, source_target_pairs={{0,1},{1,0},{2,3},{3,2},{4,5},{5,4},{6,7},{7,6},{8,9},{9,8},{10,11... | collective-permute-start | bytes 1179656 | tf_op jit(solution)/shard_map/ppermute | solution.py:210
  71.9 71.1 %collective-permute-start = (bf16[4,2,192,128]{3,2,1,0:T(8,128)(2,1)}, bf16[4,2,192,128]{3,2,1,0:T(8,128)(2,1)}, u32[]{:S(2)}, u32[]{:S(2)}) collective-permute-start(bf16[4,2,192,128]{3,2,1,0:T(8,128)(2,1)} %shard_map.39), channel_id=1, source_target_pairs={{0,1},{1,0},{2,3},{3,2},{4,5},{5,4},{6,7},{7,6},{8,9},{9,8},{10,11... | collective-permute-start | bytes 1179656 | tf_op jit(solution)/shard_map/ppermute | solution.py:210
  128.9 5.5 %copy-start = (bf16[4,2,192,128]{3,2,1,0:T(8,128)(2,1)}, bf16[4,2,192,128]{3,2,1,0:T(8,128)(2,1)S(1)}, u32[]{:S(2)}) copy-start(bf16[4,2,192,128]{3,2,1,0:T(8,128)(2,1)S(1)} %get-tuple-element.43.refs_5_.refs_1_) | copy-start | bytes 1179652
  128.9 33.4 %collective-permute-start.3 = (bf16[4,192,128]{2,1,0:T(8,128)(2,1)S(1)}, bf16[4,192,128]{2,1,0:T(8,128)(2,1)}, u32[]{:S(2)}, u32[]{:S(2)}) collective-permute-start(bf16[4,192,128]{2,1,0:T(8,128)(2,1)S(1)} %slice_bitcast_fusion), channel_id=1, source_target_pairs={{0,1},{1,0},{2,3},{3,2},{4,5},{5,4},{6,7},{7,6},{8,9},{9,8},{10,11... | collective-permute-start | bytes 589832 | tf_op jit(solution)/shard_map/ppermute | solution.py:210

commit v6 on v4

--- a/solution.py
+++ b/solution.py
@@ -254,11 +254,11 @@
     own = over(
         "y",
         attend(
-            [((mixed, 6), (mixed, 7), (far, 1)), ((far, 0), (mixed, 7), (far, 1))], 2, after=(early,)
+            [((mixed, 6), (mixed, 7), (far, 1)), ((far, 0), (mixed, 7), (far, 1))], 2, after=(frames_out,)
         ),
     )
     back = across(own[:, 1])
-    pairs = attend([((mixed, 4), (mixed, 0), (far0, 0))], 2, after=(own,))
+    pairs = attend([((mixed, 4), (mixed, 0), (far0, 0))], 2, after=(own, early))
     pairs = over("y", attend([((mixed, 5), (mixed, 2), (far1, 0))], 2, 1, pairs))
     return unpack(
         half,

time: 164 us -> 166 us (1.012)
  the two profiles are of different devices: /device:TPU:64 before, /device:TPU:8 now
where the time goes in v6:
time: 166 us; the launch traced here: 165 us
  blocking collectives  95.7 us (58%)
  starting transfers between devices  32.4 us (20%)
  Pallas kernels  22.3 us (13%)
  waiting for transfers between devices  12.7 us (8%)
  local copies, waits for them, and re-layouts  1.98 us (1%)
    all_to_all x6, blocking collectives, over(): lax.all_to_all(a, axis, split_axis=0, concat_axis=0, tiled=True)  95.7 us
    ppermute x4, starting transfers between devices, across(): return lax.ppermute(array, 'zh', [(0, 1), (1, 0)])  32.4 us
    ppermute x4, waiting for transfers between devices, across(): return lax.ppermute(array, 'zh', [(0, 1), (1, 0)])  12.7 us
    pallas_call x3, Pallas kernels, attend(): pl.pallas_call(functools.partial(attend_body, indices), grid=(1,), out_sh...  8.23 us
    pallas_call x2, Pallas kernels, pack(): pl.pallas_call(body, grid_spec=pltpu.PrefetchScalarGridSpec(num_scalar_pr...  4.46 us
    pallas_call x1, Pallas kernels, attend_frames(): pl.pallas_call(frames_body, grid=(rows // tokens,), out_shape=jax.ShapeDt...  3.71 us
  transfers between devices with their start and end apart: 4, of which 2 were waited for; matrix products, arithmetic and copies ran while one was open for 1% of the time, Pallas kernels for 11%

profile of v6, /device:TPU:8, one launch (start us, length us, event | category | flops | bytes accessed | tf_op | source)
XLA Modules:
  0.0 165.3 jit_solution(6006337006667505261)
XLA Ops:
  0.0 2.0 %shard_map.37.refs_15_ = bf16[4,3,192,128]{3,2,1,0:T(8,128)(2,1)} custom-call(s32[1]{0:T(128)} %bitcast.half_ref, bf16[1,192,3072]{2,1,0:T(8,128)(2,1)} %refs_12_.1, bf16[1,192,3072]{2,1,0:T(8,128)(2,1)} %refs_13_.1, bf16[1,192,3072]{2,1,0:T(8,128)(2,1)} %refs_14_.1), custom_call_target="tpu_custom_call" | custom-call | tf_op jit(solution)/shard_map/pallas_call | solution.py:36
  2.0 15.7 %collective-permute-start.2 = (bf16[4,3,192,128]{3,2,1,0:T(8,128)(2,1)}, bf16[4,3,192,128]{3,2,1,0:T(8,128)(2,1)S(1)}, u32[]{:S(2)}, u32[]{:S(2)}) collective-permute-start(bf16[4,3,192,128]{3,2,1,0:T(8,128)(2,1)} %shard_map.37.refs_15_), channel_id=1, source_target_pairs={{0,1},{1,0},{2,3},{3,2},{4,5},{5,4},{6,7},{7,6},{8,9},{9,8},{10,11... | collective-permute-start | bytes 1769480 | tf_op jit(solution)/shard_map/ppermute | solution.py:212
  17.8 2.4 %shard_map.38 = (bf16[4,9,192,128]{3,2,1,0:T(8,128)(2,1)S(1)}, bf16[8,3,192,128]{3,2,1,0:T(8,128)(2,1)S(1)}) custom-call(s32[1]{0:T(128)} %bitcast.half_ref, bf16[1,192,3072]{2,1,0:T(8,128)(2,1)} %refs_13_.1, bf16[1,192,3072]{2,1,0:T(8,128)(2,1)} %refs_14_.1, bf16[1,192,3072]{2,1,0:T(8,128)(2,1)} %refs_13_.1, bf16[1,192,3072]{2,1,0:T(8,128)(2,1)} %refs_14_.1, ...), custom_call_target="tpu_custom_call" | custom-call | tf_op jit(solution)/shard_map/pallas_call | solution.py:36
  20.2 25.9 %conditional.6 = (bf16[4,9,192,128]{3,2,1,0:T(8,128)(2,1)S(1)}) conditional(s32[]{:T(128)} %convert_element_type.2, bf16[4,9,192,128]{3,2,1,0:T(8,128)(2,1)S(1)} %get-tuple-element.37, bf16[4,9,192,128]{3,2,1,0:T(8,128)(2,1)S(1)} %get-tuple-element.37), branch_computations={%region_0.0_spmd, %region_1.0_spmd} | conditional | bytes 7077896 | solution.py:203
  20.2 0.1 copy.22
  20.3 25.8 %all_to_all.24 = bf16[4,9,192,128]{3,2,1,0:T(8,128)(2,1)S(1)} all-to-all(bf16[4,9,192,128]{3,2,1,0:T(8,128)(2,1)S(1)} %copy.22), channel_id=1, replica_groups=mesh['dp'=8,'tm'=8,'y'=4,'zh'=2] {'y'}, dimensions={0} | all-to-all | bytes 3538944 | tf_op jit(solution)/shard_map/cond/branch_1_fun/all_to_all | solution.py:205
  46.1 1.3 shard_map.40
  47.4 2.2 %collective-permute-start.1 = (bf16[4,2,192,128]{3,2,1,0:T(8,128)(2,1)}, bf16[4,2,192,128]{3,2,1,0:T(8,128)(2,1)}, u32[]{:S(2)}, u32[]{:S(2)}) collective-permute-start(bf16[4,2,192,128]{3,2,1,0:T(8,128)(2,1)} %shard_map.40), channel_id=1, source_target_pairs={{0,1},{1,0},{2,3},{3,2},{4,5},{5,4},{6,7},{7,6},{8,9},{9,8},{10,11... | collective-permute-start | bytes 1179656 | tf_op jit(solution)/shard_map/ppermute | solution.py:212
  49.6 21.7 %conditional.7 = (bf16[8,3,192,128]{3,2,1,0:T(8,128)(2,1)S(1)}) conditional(s32[]{:T(128)} %convert_element_type.2, bf16[8,3,192,128]{3,2,1,0:T(8,128)(2,1)S(1)} %get-tuple-element.38, bf16[8,3,192,128]{3,2,1,0:T(8,128)(2,1)S(1)} %get-tuple-element.38), branch_computations={%region_2.0_spmd, %region_3.0_spmd} | conditional | bytes 4718600 | solution.py:203
  49.6 0.1 copy.23
  49.7 21.6 %all_to_all.25 = bf16[8,3,192,128]{3,2,1,0:T(8,128)(2,1)S(1)} all-to-all(bf16[8,3,192,128]{3,2,1,0:T(8,128)(2,1)S(1)} %copy.23), channel_id=1, replica_groups=mesh['dp'=8,'tm'=8,'y'=4,'zh'=2] {'tm'}, dimensions={0} | all-to-all | bytes 2359296 | tf_op jit(solution)/shard_map/cond/branch_1_fun/all_to_all | solution.py:205
  71.3 1.3 shard_map.39
  72.7 12.3 %collective-permute-start = (bf16[4,2,192,128]{3,2,1,0:T(8,128)(2,1)}, bf16[4,2,192,128]{3,2,1,0:T(8,128)(2,1)}, u32[]{:S(2)}, u32[]{:S(2)}) collective-permute-start(bf16[4,2,192,128]{3,2,1,0:T(8,128)(2,1)} %shard_map.39), channel_id=1, source_target_pairs={{0,1},{1,0},{2,3},{3,2},{4,5},{5,4},{6,7},{7,6},{8,9},{9,8},{10,11... | collective-permute-start | bytes 1179656 | tf_op jit(solution)/shard_map/ppermute | solution.py:212
  85.0 3.7 %shard_map.41 = bf16[8,192,128]{2,1,0:T(8,128)(2,1)} custom-call(bf16[8,3,192,128]{3,2,1,0:T(8,128)(2,1)S(1)} %get-tuple-element.40.refs_0_.q_ref.k_ref.v_ref, bf16[8,3,192,128]{3,2,1,0:T(8,128)(2,1)S(1)} %get-tuple-element.40.refs_0_.q_ref.k_ref.v_ref, bf16[8,3,192,128]{3,2,1,0:T(8,128)(2,1)S(1)} %get-tuple-element.40.refs_0_.q_ref.k_ref.v_ref), custom_call_target="tpu_custom_call" | custom-call | tf_op jit(solution)/shard_map/pallas_call | solution.py:191
  88.7 13.0 %conditional.9 = (bf16[8,192,128]{2,1,0:T(8,128)(2,1)}) conditional(s32[]{:T(128)} %convert_element_type.2, bf16[8,192,128]{2,1,0:T(8,128)(2,1)} %shard_map.41, bf16[8,192,128]{2,1,0:T(8,128)(2,1)} %shard_map.41), branch_computations={%region_6.0_spmd, %region_7.0_spmd} | conditional | bytes 1572872 | solution.py:203
  88.7 1.0 copy.25
  89.7 12.0 %all_to_all.27 = bf16[8,192,128]{2,1,0:T(8,128)(2,1)} all-to-all(bf16[8,192,128]{2,1,0:T(8,128)(2,1)S(1)} %copy.25), channel_id=1, replica_groups=mesh['dp'=8,'tm'=8,'y'=4,'zh'=2] {'tm'}, dimensions={0} | all-to-all | bytes 786432 | tf_op jit(solution)/shard_map/cond/branch_1_fun/all_to_all | solution.py:205
  101.7 13.1 %conditional.8 = (bf16[4,3,192,128]{3,2,1,0:T(8,128)(2,1)S(1)}) conditional(s32[]{:T(128)} %convert_element_type.2, bf16[4,3,192,128]{3,2,1,0:T(8,128)(2,1)S(1)} %collective-permute-done.2, bf16[4,3,192,128]{3,2,1,0:T(8,128)(2,1)S(1)} %collective-permute-done.2), branch_computations={%region_4.0_spmd, %region_5.0_spmd} | conditional | bytes 2359304 | solution.py:203
  101.8 13.1 %all_to_all.26 = bf16[4,3,192,128]{3,2,1,0:T(8,128)(2,1)S(1)} all-to-all(bf16[4,3,192,128]{3,2,1,0:T(8,128)(2,1)S(1)} %copy.24), channel_id=1, replica_groups=mesh['dp'=8,'tm'=8,'y'=4,'zh'=2] {'y'}, dimensions={0} | all-to-all | bytes 1179648 | tf_op jit(solution)/shard_map/cond/branch_1_fun/all_to_all | solution.py:205
  114.9 3.0 %shard_map.42 = bf16[4,2,192,128]{3,2,1,0:T(8,128)(2,1)S(1)} custom-call(bf16[4,9,192,128]{3,2,1,0:T(8,128)(2,1)S(1)} %get-tuple-element.39.i_ref.refs_0_.refs_1_.refs_2_, bf16[4,9,192,128]{3,2,1,0:T(8,128)(2,1)S(1)} %get-tuple-element.39.i_ref.refs_0_.refs_1_.refs_2_, bf16[4,9,192,128]{3,2,1,0:T(8,128)(2,1)S(1)} %get-tuple-element.39.i_ref.refs_0_.refs_1_.refs_2_, ...), custom_call_target="tpu_custom_call" | custom-call | tf_op jit(solution)/shard_map/pallas_call | solution.py:132
  117.9 10.1 %conditional.10 = (bf16[4,2,192,128]{3,2,1,0:T(8,128)(2,1)S(1)}) conditional(s32[]{:T(128)} %convert_element_type.2, bf16[4,2,192,128]{3,2,1,0:T(8,128)(2,1)S(1)} %shard_map.42, bf16[4,2,192,128]{3,2,1,0:T(8,128)(2,1)S(1)} %shard_map.42), branch_computations={%region_8.0_spmd, %region_9.0_spmd} | conditional | bytes 1572872 | solution.py:203
  117.9 10.1 %all_to_all.28 = bf16[4,2,192,128]{3,2,1,0:T(8,128)(2,1)S(1)} all-to-all(bf16[4,2,192,128]{3,2,1,0:T(8,128)(2,1)S(1)} %copy.26), channel_id=1, replica_groups=mesh['dp'=8,'tm'=8,'y'=4,'zh'=2] {'y'}, dimensions={0} | all-to-all | bytes 786432 | tf_op jit(solution)/shard_map/cond/branch_1_fun/all_to_all | solution.py:205
  128.0 2.2 %collective-permute-start.3 = (bf16[4,192,128]{2,1,0:T(8,128)(2,1)S(1)}, bf16[4,192,128]{2,1,0:T(8,128)(2,1)S(1)}, u32[]{:S(2)}, u32[]{:S(2)}) collective-permute-start(bf16[4,192,128]{2,1,0:T(8,128)(2,1)S(1)} %slice_bitcast_fusion), channel_id=1, source_target_pairs={{0,1},{1,0},{2,3},{3,2},{4,5},{5,4},{6,7},{7,6},{8,9},{9,8},{10,11... | collective-permute-start | bytes 589832 | tf_op jit(solution)/shard_map/ppermute | solution.py:212
  130.2 0.8 shard_map.43.refs_6_.refs_3_
  131.1 2.6 %shard_map.44.refs_5_ = bf16[4,2,192,128]{3,2,1,0:T(8,128)(2,1)S(1)} custom-call(bf16[4,9,192,128]{3,2,1,0:T(8,128)(2,1)S(1)} %get-tuple-element.39.i_ref.refs_0_.refs_1_.refs_2_, bf16[4,9,192,128]{3,2,1,0:T(8,128)(2,1)S(1)} %get-tuple-element.39.i_ref.refs_0_.refs_1_.refs_2_, bf16[4,9,192,128]{3,2,1,0:T(8,128)(2,1)S(1)} %get-tuple-element.39.i_ref.refs_0_.refs_1_.refs_2_, ...), custom_call_target="tpu_custom_call" | custom-call | tf_op jit(solution)/shard_map/pallas_call | solution.py:132
  133.7 0.7 collective-permute-done.refs_3_.refs_4_
  134.4 2.6 %shard_map.45 = bf16[4,2,192,128]{3,2,1,0:T(8,128)(2,1)S(1)} custom-call(bf16[4,9,192,128]{3,2,1,0:T(8,128)(2,1)S(1)} %get-tuple-element.39.i_ref.refs_0_.refs_1_.refs_2_, bf16[4,9,192,128]{3,2,1,0:T(8,128)(2,1)S(1)} %get-tuple-element.39.i_ref.refs_0_.refs_1_.refs_2_, ...), custom_call_target="tpu_custom_call", output_to_operand_aliasing={{}: (5, {})} | custom-call | tf_op jit(solution)/shard_map/pallas_call | solution.py:132
  137.0 13.1 %conditional.11 = (bf16[4,2,192,128]{3,2,1,0:T(8,128)(2,1)S(1)}) conditional(s32[]{:T(128)} %convert_element_type.2, bf16[4,2,192,128]{3,2,1,0:T(8,128)(2,1)S(1)} %shard_map.45, bf16[4,2,192,128]{3,2,1,0:T(8,128)(2,1)S(1)} %shard_map.45), branch_computations={%region_10.0_spmd, %region_11.0_spmd} | conditional | bytes 1572872 | solution.py:203
  137.1 13.1 %all_to_all.29 = bf16[4,2,192,128]{3,2,1,0:T(8,128)(2,1)S(1)} all-to-all(bf16[4,2,192,128]{3,2,1,0:T(8,128)(2,1)S(1)} %copy.27), channel_id=1, replica_groups=mesh['dp'=8,'tm'=8,'y'=4,'zh'=2] {'y'}, dimensions={0} | all-to-all | bytes 786432 | tf_op jit(solution)/shard_map/cond/branch_1_fun/all_to_all | solution.py:205
  150.2 12.0 %collective-permute-done.3.refs_2_ = bf16[4,192,128]{2,1,0:T(8,128)(2,1)S(1)} collective-permute-done((bf16[4,192,128]{2,1,0:T(8,128)(2,1)S(1)}, bf16[4,192,128]{2,1,0:T(8,128)(2,1)S(1)}, u32[]{:S(2)}, u32[]{:S(2)}) %collective-permute-start.3) | collective-permute-done | bytes 196640 | tf_op jit(solution)/shard_map/ppermute | solution.py:212
  162.1 0.7 copy-done.1
  162.8 2.4 %shard_map.46 = bf16[1,192,3072]{2,1,0:T(8,128)(2,1)} custom-call(s32[1]{0:T(128)} %bitcast.half_ref, bf16[4,2,192,128]{3,2,1,0:T(8,128)(2,1)S(1)} %get-tuple-element.44.refs_0_, bf16[4,2,192,128]{3,2,1,0:T(8,128)(2,1)S(1)} %get-tuple-element.43.refs_5_.refs_1_, bf16[4,192,128]{2,1,0:T(8,128)(2,1)} %copy-done.1, ...), custom_call_target="tpu_custom_call", output_to_operand_aliasing={{}: (4, {})} | custom-call | tf_op jit(solution)/shard_map/pallas_call | solution.py:69
  (9 shorter events, 0.1 us)
Async XLA Ops:
  2.0 99.7 %collective-permute-start.2 = (bf16[4,3,192,128]{3,2,1,0:T(8,128)(2,1)}, bf16[4,3,192,128]{3,2,1,0:T(8,128)(2,1)S(1)}, u32[]{:S(2)}, u32[]{:S(2)}) collective-permute-start(bf16[4,3,192,128]{3,2,1,0:T(8,128)(2,1)} %shard_map.37.refs_15_), channel_id=1, source_target_pairs={{0,1},{1,0},{2,3},{3,2},{4,5},{5,4},{6,7},{7,6},{8,9},{9,8},{10,11... | collective-permute-start | bytes 1769480 | tf_op jit(solution)/shard_map/ppermute | solution.py:212
  47.4 83.6 %collective-permute-start.1 = (bf16[4,2,192,128]{3,2,1,0:T(8,128)(2,1)}, bf16[4,2,192,128]{3,2,1,0:T(8,128)(2,1)}, u32[]{:S(2)}, u32[]{:S(2)}) collective-permute-start(bf16[4,2,192,128]{3,2,1,0:T(8,128)(2,1)} %shard_map.40), channel_id=1, source_target_pairs={{0,1},{1,0},{2,3},{3,2},{4,5},{5,4},{6,7},{7,6},{8,9},{9,8},{10,11... | collective-permute-start | bytes 1179656 | tf_op jit(solution)/shard_map/ppermute | solution.py:212
  72.7 61.7 %collective-permute-start = (bf16[4,2,192,128]{3,2,1,0:T(8,128)(2,1)}, bf16[4,2,192,128]{3,2,1,0:T(8,128)(2,1)}, u32[]{:S(2)}, u32[]{:S(2)}) collective-permute-start(bf16[4,2,192,128]{3,2,1,0:T(8,128)(2,1)} %shard_map.39), channel_id=1, source_target_pairs={{0,1},{1,0},{2,3},{3,2},{4,5},{5,4},{6,7},{7,6},{8,9},{9,8},{10,11... | collective-permute-start | bytes 1179656 | tf_op jit(solution)/shard_map/ppermute | solution.py:212
  101.7 13.1 %copy-start = (bf16[8,192,128]{2,1,0:T(8,128)(2,1)S(1)}, bf16[8,192,128]{2,1,0:T(8,128)(2,1)}, u32[]{:S(2)}) copy-start(bf16[8,192,128]{2,1,0:T(8,128)(2,1)} %get-tuple-element.42.refs_6_.refs_0_) | copy-start | bytes 1179652
  128.0 34.1 %collective-permute-start.3 = (bf16[4,192,128]{2,1,0:T(8,128)(2,1)S(1)}, bf16[4,192,128]{2,1,0:T(8,128)(2,1)S(1)}, u32[]{:S(2)}, u32[]{:S(2)}) collective-permute-start(bf16[4,192,128]{2,1,0:T(8,128)(2,1)S(1)} %slice_bitcast_fusion), channel_id=1, source_target_pairs={{0,1},{1,0},{2,3},{3,2},{4,5},{5,4},{6,7},{7,6},{8,9},{9,8},{10,11... | collective-permute-start | bytes 589832 | tf_op jit(solution)/shard_map/ppermute | solution.py:212
  162.1 0.7 copy-start.1
